TPU v7x, 32 devices: a whole 2x2x4 slice. The times are simulated.
32 devices in a mesh: loop: 8 (over y, x, core), dp: 4 (over z).
Axes of the slice: x: 2, y: 2, z: 4, core: 2. Of those that a mesh axis runs over, the one named last changes fastest.
Arguments:
- image_raw: bfloat16 [4, 1024, 1152], P('dp', 'loop'), may hold values from -0.19921875 to 0.19921875
- text_feat: bfloat16 [4, 1024, 1152], P('dp', 'loop'), may hold values from -6 to 6
- text_head: bfloat16 [1152, 1152], replicated, may hold values from -0.1875 to 0.1875
- image_of_pair: int32 [4, 1024], P('dp', 'loop'), may hold values from 0 to 255, as said below
- logit_scale: float32 [], replicated, may hold values from 10 to 30
- logit_bias: float32 [], replicated, may hold values from -3 to -1
Outputs:
- d_text_feat: float32 [4, 1024, 1152], P('dp', 'loop')
- d_image: float32 [8, 256, 1152], P('loop', 'dp')
Inputs may be any that keep to these rules, and one draw needn't show every extreme that they name: `image_of_pair`: pair row i of a replica belongs to column i // 128. Every image of a column is named by 1 to 5 pairs of that column over all replicas. Image m of a column is owned by the device of that column's loop index and dp index m // 64. The pairs of one device name images of one owner at most 80 times; in every draw some owner receives exactly 80 from every device of its column.
All inputs are finite; a program needn't handle non-finite values.
Results may differ from a plain program's by a relative error of at most 0.0057.
Values may be sent and summed in bfloat16 or wider, within the bound.
A program may use at most 64 MiB of HBM per device.

v0:
```python
import jax
import jax.numpy as jnp
from jax import lax
from jax.sharding import PartitionSpec as P

LEVELS = 3


EPS = 1e-06


def from_partner(value, axis, apart):
    mask = 2**apart
    pairs = [(source, source ^ mask) for source in range(lax.axis_size(axis))]
    return lax.ppermute(value, axis, pairs)


def unit_rows(values):
    inv = lax.rsqrt(jnp.sum(values * values, axis=-1, keepdims=True) + EPS)
    return (values * inv, inv)


def pair_weights(left, right, same, scale, shift):
    logits = (
        scale
        * lax.dot_general(left, right, (((1,), (1,)), ((), ())), preferred_element_type=jnp.float32)
        + shift
    )
    sign = jnp.where(same, jnp.float32(1.0), jnp.float32(-1.0))
    return (-sign * jax.nn.sigmoid(-sign * logits)).astype(jnp.bfloat16)


def left_product(weight, block):
    return lax.dot_general(
        weight, block, (((0,), (0,)), ((), ())), preferred_element_type=jnp.float32
    )


def shards(image_raw, text_feat, text_head, image_of_pair, logit_scale, logit_bias):
    rows = image_raw.shape[1]
    width = image_raw.shape[2]
    unit_x, inv_x = unit_rows(image_raw[0].astype(jnp.float32))
    image_emb = unit_x.astype(jnp.bfloat16)
    text_pre = jnp.dot(text_feat[0], text_head, preferred_element_type=jnp.float32)
    unit_y, inv_y = unit_rows(text_pre)
    text_emb = unit_y.astype(jnp.bfloat16)
    labels = image_of_pair[0]
    group = 2**LEVELS
    position = lax.axis_index("loop") % group
    same_home = labels[:, None] == labels[None, :]
    w_home = pair_weights(image_emb, text_emb, same_home, logit_scale, logit_bias)
    img_grad = logit_scale * jnp.dot(w_home, text_emb, preferred_element_type=jnp.float32)
    txt_grad = logit_scale * left_product(w_home, image_emb)
    held = jnp.stack([image_emb, text_emb])
    for level in range(LEVELS):
        far = from_partner(held, "loop", level)
        far_x = far[0]
        far_y = far[1]
        apart = jnp.zeros((rows, far_y.shape[0]), jnp.bool_)
        w_image = pair_weights(image_emb, far_y, apart, logit_scale, logit_bias)
        img_grad = img_grad + logit_scale * jnp.dot(
            w_image, far_y, preferred_element_type=jnp.float32
        )
        w_text = pair_weights(far_x, text_emb, apart.T, logit_scale, logit_bias)
        txt_grad = txt_grad + logit_scale * left_product(w_text, far_x)
        if level + 1 < LEVELS:
            lower = position // 2**level % 2 == 0
            held = jnp.where(
                lower, jnp.concatenate([held, far], axis=1), jnp.concatenate([far, held], axis=1)
            )
    d_image_pair = (img_grad - unit_x * jnp.sum(unit_x * img_grad, axis=-1, keepdims=True)) * inv_x
    d_text_pre = (
        (txt_grad - unit_y * jnp.sum(unit_y * txt_grad, axis=-1, keepdims=True)) * inv_y
    ).astype(jnp.bfloat16)
    d_text_feat = lax.dot_general(
        d_text_pre, text_head, (((1,), (1,)), ((), ())), preferred_element_type=jnp.float32
    )
    owners = lax.axis_size("dp")
    images_dev = rows // 2
    table_ids = jnp.arange(images_dev * owners, dtype=jnp.int32)
    onehot = (table_ids[:, None] == labels[None, :]).astype(jnp.float32)
    table = jnp.dot(onehot, d_image_pair, precision=lax.Precision.HIGHEST).reshape(
        owners, images_dev, width
    )
    arrived = lax.all_to_all(table, "dp", split_axis=0, concat_axis=0, tiled=True)
    d_image = jnp.sum(arrived, axis=0)
    return (d_text_feat[None], d_image[None])


def solution(mesh):
    placed = (P("dp", "loop", None), P("dp", "loop", None), P(), P("dp", "loop"), P(), P())
    return jax.shard_map(
        shards,
        mesh=mesh,
        in_specs=placed,
        out_specs=(P("dp", "loop", None), P("loop", "dp", None)),
        check_vma=False,
    )
```

profile of v0, /device:TPU:0, one launch (start us, length us, event | category | flops | bytes accessed | tf_op | source)
XLA Modules:
  0.0 141.4 jit_solution(9363942446883686713)
XLA Ops:
  0.6 0.0 copy-start
  0.6 0.0 copy-start.1
  0.7 1.7 %copy-done = bf16[1152,1152]{1,0:T(8,128)(2,1)S(1)} copy-done((bf16[1152,1152]{1,0:T(8,128)(2,1)S(1)}, bf16[1152,1152]{1,0:T(8,128)(2,1)}, u32[]{:S(2)}) %copy-start) | copy-done | bytes 2654232
  2.4 1.6 %multiply_reduce_fusion.1 = (f32[128]{0:T(128)S(1)}, f32[128,1152]{1,0:T(8,128)S(1)}) fusion(bf16[1152,1152]{1,0:T(8,128)(2,1)S(1)} %copy-done, bf16[1,128,1152]{2,1,0:T(8,128)(2,1)} %param.7), kind=kOutput, calls=%fused_computation.84 | convolution fusion | flops 340033408 | bytes 3539456 | tf_op jit(solution)/shard_map/dot_general | solution.py:44
  4.1 0.0 copy-done.1
  4.1 0.1 fusion.60
  4.2 0.1 fusion.61
  4.3 0.0 copy-start.5
  4.4 0.1 fusion.120
  4.5 0.0 copy-start.4
  4.5 0.7 copy-done.4
  5.2 0.9 pad_maximum_fusion
  6.1 0.0 copy-done.5
  6.1 0.4 collective-permute-start
  6.5 2.0 %collective-permute-done = bf16[2,128,1152]{2,1,0:T(8,128)(2,1)} collective-permute-done((bf16[2,128,1152]{2,1,0:T(8,128)(2,1)}, bf16[2,128,1152]{2,1,0:T(8,128)(2,1)}, u32[]{:S(2)}, u32[]{:S(2)}) %collective-permute-start) | collective-permute-done | bytes 589856 | tf_op jit(solution)/shard_map/ppermute | solution.py:15
  8.5 2.9 %maximum_select_fusion.1 = bf16[2,256,1152]{2,1,0:T(8,128)(2,1)} fusion(bf16[2,128,1152]{2,1,0:T(8,128)(2,1)} %collective-permute-done, bf16[1,128,1152]{2,1,0:T(8,128)(2,1)} %copy-done.4, bf16[1,128,1152]{2,1,0:T(8,128)(2,1)} %copy-done.5, pred[]{:T(512)S(6)} %eq.42), kind=kLoop, calls=%fused_computation.12 | loop fusion | flops 7667712 | bytes 2359297 | tf_op jit(solution)/shard_map/jit(_where)/select_n | solution.py:68
  11.4 2.9 %collective-permute-start.1 = (bf16[2,256,1152]{2,1,0:T(8,128)(2,1)}, bf16[2,256,1152]{2,1,0:T(8,128)(2,1)}, u32[]{:S(2)}, u32[]{:S(2)}) collective-permute-start(bf16[2,256,1152]{2,1,0:T(8,128)(2,1)} %maximum_select_fusion.1), channel_id=1, source_target_pairs={{0,8},{4,12},{8,0},{12,4},{16,24},{20,28},{24,16},{28,20},{1,9},{5... | collective-permute-start | bytes 3538952 | tf_op jit(solution)/shard_map/ppermute | solution.py:15
  14.3 0.0 copy-start.7
  14.3 26.6 %collective-permute-done.1 = bf16[2,256,1152]{2,1,0:T(8,128)(2,1)} collective-permute-done((bf16[2,256,1152]{2,1,0:T(8,128)(2,1)}, bf16[2,256,1152]{2,1,0:T(8,128)(2,1)}, u32[]{:S(2)}, u32[]{:S(2)}) %collective-permute-start.1) | collective-permute-done | bytes 1179680 | tf_op jit(solution)/shard_map/ppermute | solution.py:15
  40.9 3.9 %maximum_select_fusion = bf16[2,512,1152]{2,1,0:T(8,128)(2,1)} fusion(bf16[2,256,1152]{2,1,0:T(8,128)(2,1)} %collective-permute-done.1, bf16[2,256,1152]{2,1,0:T(8,128)(2,1)} %maximum_select_fusion.1, pred[]{:T(512)S(6)} %eq.43), kind=kLoop, calls=%fused_computation.9 | loop fusion | flops 10616832 | bytes 4718593 | tf_op jit(solution)/shard_map/jit(_where)/select_n | solution.py:68
  44.8 1.8 %collective-permute-start.2 = (bf16[2,512,1152]{2,1,0:T(8,128)(2,1)}, bf16[2,512,1152]{2,1,0:T(8,128)(2,1)}, u32[]{:S(2)}, u32[]{:S(2)}) collective-permute-start(bf16[2,512,1152]{2,1,0:T(8,128)(2,1)} %maximum_select_fusion), channel_id=1, source_target_pairs={{0,16},{4,20},{8,24},{12,28},{16,0},{20,4},{24,8},{28,12},{1,17},{... | collective-permute-start | bytes 7077896 | tf_op jit(solution)/shard_map/ppermute | solution.py:15
  47.9 0.1 multiply_convert_fusion.1
  48.0 0.0 copy-start.2
  48.0 0.0 copy-done.7
  48.0 0.3 fusion.47
  48.4 0.4 copy-done.2
  48.7 0.0 copy-start.6
  48.7 0.6 copy-done.6
  49.3 1.0 fusion.110
  50.4 2.7 %convolution_add_fusion.1 = f32[128,1152]{1,0:T(8,128)} fusion(f32[128,1152]{1,0:T(8,128)} %fusion.110, bf16[2,128,1152]{2,1,0:T(8,128)(2,1)} %collective-permute-done, f32[]{:T(128)S(6)} %copy.9, f32[]{:T(128)S(6)} %copy.8, bf16[1,128,1152]{2,1,0:T(8,128)(2,1)S(1)} %copy-done.1, f32[128]{0:T(128)S(1)} %add_rsqrt_fusion.1), kind=kOutput, calls=%fused_computation.3 | convolution fusion | flops 76185600 | bytes 2064904 | tf_op jit(solution)/shard_map/dot_general | solution.py:61
  53.0 44.9 %collective-permute-done.2 = bf16[2,512,1152]{2,1,0:T(8,128)(2,1)} collective-permute-done((bf16[2,512,1152]{2,1,0:T(8,128)(2,1)}, bf16[2,512,1152]{2,1,0:T(8,128)(2,1)}, u32[]{:S(2)}, u32[]{:S(2)}) %collective-permute-start.2) | collective-permute-done | bytes 2359328 | tf_op jit(solution)/shard_map/ppermute | solution.py:15
  97.9 3.4 %fusion.27 = f32[128,1152]{1,0:T(8,128)} fusion(bf16[2,512,1152]{2,1,0:T(8,128)(2,1)} %collective-permute-done.2, f32[]{:T(128)S(6)} %copy.9, f32[]{:T(128)S(6)} %copy.8, bf16[1,128,1152]{2,1,0:T(8,128)(2,1)S(1)} %copy-done.1, f32[128]{0:T(128)S(1)} %add_rsqrt_fusion.1), kind=kOutput, calls=%fused_computation.40 | convolution fusion | flops 302825472 | bytes 3244552 | tf_op jit(solution)/shard_map/dot_general | solution.py:61
  101.3 3.1 %fusion.55 = (f32[128]{0:T(128)S(1)}, f32[128,1152]{1,0:T(8,128)}) fusion(bf16[1,128,1152]{2,1,0:T(8,128)(2,1)S(1)} %copy-done.1, f32[128]{0:T(128)S(1)} %add_rsqrt_fusion.1, f32[]{:T(128)S(6)} %copy.8, f32[128,1152]{1,0:T(8,128)} %fusion.27, f32[128,1152]{1,0:T(8,128)} %convolution_add_fusion.1, bf16[2,256,1152]{2,1,0:T(8,128)(2,1)} %collective-permute-done.1, ...), kind=kOutput, calls=%fused_computation.73 | convolution fusion | flops 152665984 | bytes 3542016 | tf_op jit(solution)/shard_map/dot_general | solution.py:61
  104.4 2.9 %fusion.58 = f32[256,1152]{1,0:T(8,128)} fusion(f32[128,1152]{1,0:T(8,128)} %get-tuple-element.7, bf16[1,128,1152]{2,1,0:T(8,128)(2,1)S(1)} %copy-done.1, f32[128]{0:T(128)S(1)} %get-tuple-element.6, f32[128]{0:T(128)S(1)} %add_rsqrt_fusion.1, s32[128]{0:T(128)S(1)} %bitcast.91), kind=kOutput, calls=%fused_computation.76 | convolution fusion | flops 453754880 | bytes 2065920 | tf_op jit(solution)/shard_map/dot_general | solution.py:82
  107.3 4.8 %all-to-all-start = ((f32[4,64,1152]{2,1,0:T(8,128)}), f32[4,64,1152]{2,1,0:T(8,128)}, u32[]{:S(2)}, u32[]{:S(2)}) async-start(f32[4,64,1152]{2,1,0:T(8,128)} %bitcast.88), calls=%async_computation | async-start | bytes 2359296 | tf_op jit(solution)/shard_map/all_to_all | solution.py:85
  112.1 1.9 %fusion.80 = f32[128,1152]{1,0:T(8,128)} fusion(bf16[128,128]{1,0:T(8,128)(2,1)} %copy-done.6, bf16[1,128,1152]{2,1,0:T(8,128)(2,1)S(1)} %copy-done.1, f32[128]{0:T(128)S(1)} %add_rsqrt_fusion.1), kind=kOutput, calls=%fused_computation.104 | convolution fusion | flops 38191104 | bytes 918016 | tf_op jit(solution)/shard_map/dot_general | solution.py:34
  114.0 2.8 %convolution_add_fusion.3 = f32[128,1152]{1,0:T(8,128)} fusion(f32[128,1152]{1,0:T(8,128)} %fusion.80, bf16[128,1152]{1,0:T(8,128)(2,1)} %copy-done.2, bf16[2,128,1152]{2,1,0:T(8,128)(2,1)} %collective-permute-done, f32[]{:T(128)S(6)} %copy.9, f32[]{:T(128)S(6)} %copy.8), kind=kOutput, calls=%fused_computation.7 | convolution fusion | flops 75743232 | bytes 2064392 | tf_op jit(solution)/shard_map/dot_general | solution.py:34
  116.7 0.0 copy-start.3
  116.7 3.6 %fusion.26 = f32[128,1152]{1,0:T(8,128)} fusion(bf16[128,1152]{1,0:T(8,128)(2,1)} %copy-done.2, bf16[2,512,1152]{2,1,0:T(8,128)(2,1)} %collective-permute-done.2, f32[]{:T(128)S(6)} %copy.9, f32[]{:T(128)S(6)} %copy.8), kind=kOutput, calls=%fused_computation.39 | convolution fusion | flops 302383104 | bytes 3244040 | tf_op jit(solution)/shard_map/dot_general | solution.py:34
  120.4 0.0 copy-done.3
  120.4 3.2 %multiply_reduce_fusion = (f32[128]{0:T(128)S(1)}, f32[128,1152]{1,0:T(8,128)}) fusion(f32[128,1152]{1,0:T(8,128)S(1)} %get-tuple-element.3, f32[128]{0:T(128)S(1)} %add_rsqrt_fusion, f32[]{:T(128)S(6)} %copy.8, f32[128,1152]{1,0:T(8,128)} %fusion.26, f32[128,1152]{1,0:T(8,128)} %convolution_add_fusion.3, bf16[2,256,1152]{2,1,0:T(8,128)(2,1)} %collective-permute-done.1, ...), kind=kOutput, calls=%fused_computation.83 | convolution fusion | flops 152076160 | bytes 3836416 | tf_op jit(solution)/shard_map/dot_general | solution.py:34
  123.6 2.8 %convolution_bitcast_fusion = f32[1,128,1152]{2,1,0:T(8,128)} fusion(bf16[1152,1152]{1,0:T(8,128)(2,1)S(1)} %copy-done, f32[128,1152]{1,0:T(8,128)} %get-tuple-element.5, f32[128,1152]{1,0:T(8,128)S(1)} %get-tuple-element.3, f32[128]{0:T(128)S(1)} %get-tuple-element.4, f32[128]{0:T(128)S(1)} %add_rsqrt_fusion), kind=kOutput, calls=%fused_computation.8 | convolution fusion | flops 340475904 | bytes 4424704 | tf_op jit(solution)/shard_map/dot_general | solution.py:75
  126.4 13.0 %all-to-all-done = f32[4,64,1152]{2,1,0:T(8,128)} async-done(((f32[4,64,1152]{2,1,0:T(8,128)}), f32[4,64,1152]{2,1,0:T(8,128)}, u32[]{:S(2)}, u32[]{:S(2)}) %all-to-all-start) | async-done | bytes 1179680 | tf_op jit(solution)/shard_map/all_to_all | solution.py:85
  139.3 2.1 %reduce_sum.49 = f32[64,1152]{1,0:T(8,128)} reduce(f32[4,64,1152]{2,1,0:T(8,128)} %all-to-all-done, f32[]{:T(128)} %constant.67.clone.1), dimensions={0}, to_apply=%region_4.5 | reduce | flops 221184 | bytes 1474564 | tf_op jit(solution)/shard_map/reduce_sum | solution.py:86
  (2 shorter events, 0.0 us)
Async XLA Ops:
  0.6 1.8 %copy-start = (bf16[1152,1152]{1,0:T(8,128)(2,1)S(1)}, bf16[1152,1152]{1,0:T(8,128)(2,1)}, u32[]{:S(2)}) copy-start(bf16[1152,1152]{1,0:T(8,128)(2,1)} %param.8) | copy-start | bytes 7962628
  0.6 3.4 %copy-start.1 = (bf16[1,128,1152]{2,1,0:T(8,128)(2,1)S(1)}, bf16[1,128,1152]{2,1,0:T(8,128)(2,1)}, u32[]{:S(2)}) copy-start(bf16[1,128,1152]{2,1,0:T(8,128)(2,1)} %param.6) | copy-start | bytes 884740
  4.3 1.7 %copy-start.5 = (bf16[1,128,1152]{2,1,0:T(8,128)(2,1)}, bf16[1,128,1152]{2,1,0:T(8,128)(2,1)S(1)}, u32[]{:S(2)}) copy-start(bf16[1,128,1152]{2,1,0:T(8,128)(2,1)S(1)} %fusion.61) | copy-start | bytes 884740
  4.5 0.7 copy-start.4
  6.1 2.4 %collective-permute-start = (bf16[2,128,1152]{2,1,0:T(8,128)(2,1)}, bf16[2,128,1152]{2,1,0:T(8,128)(2,1)}, u32[]{:S(2)}, u32[]{:S(2)}) collective-permute-start(bf16[2,128,1152]{2,1,0:T(8,128)(2,1)} %pad_maximum_fusion), channel_id=1, source_target_pairs={{0,4},{4,0},{8,12},{12,8},{16,20},{20,16},{24,28},{28,24},{1,5},{5... | collective-permute-start | bytes 1769480 | tf_op jit(solution)/shard_map/ppermute | solution.py:15
  11.4 29.4 %collective-permute-start.1 = (bf16[2,256,1152]{2,1,0:T(8,128)(2,1)}, bf16[2,256,1152]{2,1,0:T(8,128)(2,1)}, u32[]{:S(2)}, u32[]{:S(2)}) collective-permute-start(bf16[2,256,1152]{2,1,0:T(8,128)(2,1)} %maximum_select_fusion.1), channel_id=1, source_target_pairs={{0,8},{4,12},{8,0},{12,4},{16,24},{20,28},{24,16},{28,20},{1,9},{5... | collective-permute-start | bytes 3538952 | tf_op jit(solution)/shard_map/ppermute | solution.py:15
  14.3 33.7 %copy-start.7 = (s32[1,128]{1,0:T(1,128)S(1)}, s32[1,128]{1,0:T(1,128)}, u32[]{:S(2)}) copy-start(s32[1,128]{1,0:T(1,128)} %param.9) | copy-start | bytes 1540
  44.8 53.1 %collective-permute-start.2 = (bf16[2,512,1152]{2,1,0:T(8,128)(2,1)}, bf16[2,512,1152]{2,1,0:T(8,128)(2,1)}, u32[]{:S(2)}, u32[]{:S(2)}) collective-permute-start(bf16[2,512,1152]{2,1,0:T(8,128)(2,1)} %maximum_select_fusion), channel_id=1, source_target_pairs={{0,16},{4,20},{8,24},{12,28},{16,0},{20,4},{24,8},{28,12},{1,17},{... | collective-permute-start | bytes 7077896 | tf_op jit(solution)/shard_map/ppermute | solution.py:15
  48.0 0.7 copy-start.2
  48.7 0.6 copy-start.6
  107.3 32.0 %all-to-all-start = ((f32[4,64,1152]{2,1,0:T(8,128)}), f32[4,64,1152]{2,1,0:T(8,128)}, u32[]{:S(2)}, u32[]{:S(2)}) async-start(f32[4,64,1152]{2,1,0:T(8,128)} %bitcast.88), calls=%async_computation | async-start | bytes 2359296 | tf_op jit(solution)/shard_map/all_to_all | solution.py:85
  116.7 3.6 %copy-start.3 = (bf16[128,1152]{1,0:T(8,128)(2,1)S(1)}, bf16[128,1152]{1,0:T(8,128)(2,1)}, u32[]{:S(2)}) copy-start(bf16[128,1152]{1,0:T(8,128)(2,1)} %copy-done.2) | copy-start | bytes 884740
where the time goes:
time: 142 us; the launch traced here: 141 us
  waiting for transfers between devices  86.4 us (61%)
  matrix products  29.3 us (21%)
  other arithmetic  10.3 us (7%)
  starting transfers between devices  9.89 us (7%)
  local copies, waits for them, and re-layouts  3.45 us (2%)
  between operations  2.05 us (1%)
    ppermute x3, waiting for transfers between devices, from_partner(): return lax.ppermute(value, axis, pairs)  73.4 us
    all_to_all x1, waiting for transfers between devices, shards(): lax.all_to_all(table, 'dp', split_axis=0, concat_axis=0, tiled=True)  13 us
    dot_general x4, matrix products, left_product(): lax.dot_general(weight, block, (((0,), (0,)), ((), ())), preferred_elemen...  11.5 us
    dot_general x3, matrix products, shards(): jnp.dot(w_image, far_y, preferred_element_type=jnp.float32)  9.15 us
    select_n x2, other arithmetic, shards(): jnp.where(lower, jnp.concatenate([held, far], axis=1), jnp.concatenate([f...  6.88 us
    ppermute x3, starting transfers between devices, from_partner(): return lax.ppermute(value, axis, pairs)  5.08 us
    all_to_all x1, starting transfers between devices, shards(): lax.all_to_all(table, 'dp', split_axis=0, concat_axis=0, tiled=True)  4.81 us
    unnamed x16, local copies, waits for them, and re-layouts  3.45 us
  transfers between devices with their start and end apart: 4, of which 4 were waited for; matrix products, arithmetic and copies ran while one was open for 13% of the time, Pallas kernels for 0%

commit v1 on v0

v1 whole, which is shorter than its diff:
```python
import functools

import jax
import jax.numpy as jnp
from jax import lax
from jax.experimental import pallas as pl
from jax.experimental.pallas import tpu as pltpu
from jax.sharding import PartitionSpec as P

EPS = 1e-06
POOL_DEVS = 8
CORE, NEAR, FAR = 1, 2, 4
NT = (((1,), (1,)), ((), ()))


def partner(me, mask):
    bit = lax.rem(lax.div(me, mask), 2)
    return me + mask * (1 - 2 * bit)


class Spread:
    def __init__(self, buf, send, recv, me, rows):
        half = rows // 2
        peers = {m: partner(me, m) for m in (CORE, NEAR, FAR)}

        def copy(at, slot, mask, first, count):
            source = buf.at[pl.ds(slot * rows + first, count)]
            target = buf.at[pl.ds((slot ^ mask) * rows + first, count)]
            return pltpu.make_async_remote_copy(
                src_ref=source,
                dst_ref=target,
                send_sem=send.at[at],
                recv_sem=recv.at[at],
                device_id={"loop": peers[mask]},
                device_id_type=pl.DeviceIdType.MESH,
            )

        self.own_core = copy(0, 0, CORE, 0, rows)
        self.near_a = copy(1, 0, NEAR, 0, half)
        self.near_b = copy(2, 0, NEAR, half, half)
        self.far_a = copy(3, 0, FAR, 0, half)
        self.far_b = copy(4, 0, FAR, half, half)
        self.diag_a = copy(5, NEAR, FAR, 0, half)
        self.diag_b = copy(6, FAR, NEAR, half, half)
        self.near_core = copy(7, NEAR, CORE, 0, rows)
        self.far_core = copy(8, FAR, CORE, 0, rows)
        self.diag_core_a = copy(9, NEAR | FAR, CORE, 0, half)
        self.diag_core_b = copy(10, NEAR | FAR, CORE, half, half)


COPIES = 11


def kernel(
    owners,
    scale_ref,
    shift_ref,
    label_ref,
    image_ref,
    feat_ref,
    head_ref,
    d_feat_ref,
    d_image_ref,
    image_v,
    feat_v,
    head_v,
    xbuf,
    ybuf,
    unit_y_v,
    d_pair_v,
    d_feat_v,
    table_out,
    table_in,
    load_sem,
    store_sem,
    x_send,
    x_recv,
    y_send,
    y_recv,
    t_send,
    t_recv,
):
    rows, width = image_v.shape
    images = table_out.shape[1]
    me = lax.axis_index("loop")
    owner = lax.axis_index("dp")

    load_image = pltpu.make_async_copy(image_ref.at[0], image_v, load_sem.at[0])
    load_feat = pltpu.make_async_copy(feat_ref.at[0], feat_v, load_sem.at[1])
    load_head = pltpu.make_async_copy(head_ref, head_v, load_sem.at[2])
    load_image.start()
    load_feat.start()
    load_head.start()

    barrier = pltpu.get_barrier_semaphore()
    for mask in (CORE, NEAR, FAR):
        pl.semaphore_signal(
            barrier, inc=1, device_id={"loop": partner(me, mask)}, device_id_type=pl.DeviceIdType.MESH
        )
    for apart in range(1, owners):
        pl.semaphore_signal(
            barrier,
            inc=1,
            device_id={"dp": lax.rem(owner + apart, owners)},
            device_id_type=pl.DeviceIdType.MESH,
        )

    scale = scale_ref[0]
    shift = shift_ref[0]
    label_row = label_ref[...].astype(jnp.float32)
    label_grid = jnp.broadcast_to(label_row, (rows, rows))
    same = label_grid == label_grid.T

    xs = Spread(xbuf, x_send, x_recv, me, rows)
    ys = Spread(ybuf, y_send, y_recv, me, rows)

    load_image.wait()
    image = image_v[...].astype(jnp.float32)
    inv_x = lax.rsqrt(jnp.sum(image * image, axis=-1, keepdims=True) + EPS)
    xbuf[pl.ds(0, rows)] = (image * inv_x).astype(jnp.bfloat16)

    pl.semaphore_wait(barrier, 3 + owners - 1)
    xs.near_a.start()
    xs.far_b.start()
    xs.own_core.start()

    load_feat.wait()
    load_head.wait()
    text_pre = jnp.dot(feat_v[...], head_v[...], preferred_element_type=jnp.float32)
    inv_y = lax.rsqrt(jnp.sum(text_pre * text_pre, axis=-1, keepdims=True) + EPS)
    unit_y = text_pre * inv_y
    unit_y_v[...] = unit_y
    ybuf[pl.ds(0, rows)] = unit_y.astype(jnp.bfloat16)
    ys.near_a.start()
    ys.far_b.start()
    ys.near_b.start()
    ys.far_a.start()
    ys.own_core.start()

    def part(mine, buf, group):
        block = buf[pl.ds(group * 2 * rows, 2 * rows)]
        logits = scale * lax.dot_general(mine, block, NT, preferred_element_type=jnp.float32) + shift
        if group == 0:
            flip = jnp.concatenate([same, jnp.zeros_like(same)], axis=1)
            value = jax.nn.sigmoid(jnp.where(flip, -logits, logits))
            value = jnp.where(flip, -value, value)
        else:
            value = jax.nn.sigmoid(logits)
        return jnp.dot(value.astype(jnp.bfloat16), block, preferred_element_type=jnp.float32)

    x_own = xbuf[pl.ds(0, rows)]
    y_own = ybuf[pl.ds(0, rows)]

    ys.own_core.wait_recv()
    total = part(x_own, ybuf, 0)
    ys.near_a.wait_recv()
    ys.diag_a.start()
    ys.far_b.wait_recv()
    ys.diag_b.start()
    ys.near_b.wait_recv()
    ys.near_core.start()
    ys.far_a.wait_recv()
    ys.far_core.start()
    ys.diag_a.wait_send()
    ys.diag_b.wait_send()
    xs.near_b.start()
    xs.far_a.start()
    xs.near_a.wait_recv()
    xs.diag_a.start()
    xs.far_b.wait_recv()
    xs.diag_b.start()
    ys.near_core.wait_recv()
    total = total + part(x_own, ybuf, 1)
    ys.far_core.wait_recv()
    total = total + part(x_own, ybuf, 2)
    ys.diag_a.wait_recv()
    ys.diag_core_a.start()
    ys.diag_b.wait_recv()
    ys.diag_core_b.start()
    ys.diag_core_a.wait_recv()
    ys.diag_core_b.wait_recv()
    total = total + part(x_own, ybuf, 3)
    grad = scale * total
    unit_x = image * inv_x
    d_pair = (grad - unit_x * jnp.sum(unit_x * grad, axis=-1, keepdims=True)) * inv_x
    d_pair_v[...] = d_pair.astype(jnp.bfloat16)

    def table(apart):
        first = (lax.rem(owner + apart, owners) * images).astype(jnp.float32)
        ids = lax.broadcasted_iota(jnp.int32, (images, rows), 0).astype(jnp.float32) + first
        onehot = jnp.where(ids == label_row, 1.0, 0.0).astype(jnp.bfloat16)
        return jnp.dot(onehot, d_pair_v[...], preferred_element_type=jnp.float32)

    tables = []
    order = sorted(range(1, owners), key=lambda apart: (-min(apart, owners - apart), apart))
    for apart in order:
        table_out[apart] = table(apart).astype(jnp.bfloat16)
        send = pltpu.make_async_remote_copy(
            src_ref=table_out.at[apart],
            dst_ref=table_in.at[apart],
            send_sem=t_send.at[apart],
            recv_sem=t_recv.at[apart],
            device_id={"dp": lax.rem(owner + apart, owners)},
            device_id_type=pl.DeviceIdType.MESH,
        )
        send.start()
        tables.append((apart, send))
    d_image_ref[0] = table(0)

    xs.near_b.wait_recv()
    xs.near_core.start()
    xs.far_a.wait_recv()
    xs.far_core.start()
    xs.own_core.wait_recv()
    total = part(y_own, xbuf, 0)
    xs.near_core.wait_recv()
    total = total + part(y_own, xbuf, 1)
    xs.far_core.wait_recv()
    total = total + part(y_own, xbuf, 2)
    xs.diag_a.wait_recv()
    xs.diag_core_a.start()
    xs.diag_b.wait_recv()
    xs.diag_core_b.start()
    xs.diag_core_a.wait_recv()
    xs.diag_core_b.wait_recv()
    total = total + part(y_own, xbuf, 3)
    grad = scale * total
    unit_y = unit_y_v[...]
    d_text = (grad - unit_y * jnp.sum(unit_y * grad, axis=-1, keepdims=True)) * inv_y
    d_feat_v[...] = lax.dot_general(
        d_text.astype(jnp.bfloat16), head_v[...], NT, preferred_element_type=jnp.float32
    )
    store = pltpu.make_async_copy(d_feat_v, d_feat_ref.at[0], store_sem)
    store.start()

    for apart, send in tables:
        send.wait_recv()
        d_image_ref[0] += table_in[apart].astype(jnp.float32)

    store.wait()
    for spread in (xs, ys):
        for name, copy in vars(spread).items():
            if spread is xs or name not in ("diag_a", "diag_b"):
                copy.wait_send()
    for _, send in tables:
        send.wait_send()


def shards(owners, image_raw, text_feat, text_head, image_of_pair, logit_scale, logit_bias):
    _, rows, width = image_raw.shape
    depth = text_head.shape[0]
    images = rows // 2
    anywhere = pl.BlockSpec(memory_space=pl.ANY)
    scalar = pl.BlockSpec(memory_space=pltpu.SMEM)
    vmem = pl.BlockSpec(memory_space=pltpu.VMEM)
    dma = pltpu.SemaphoreType.DMA
    return pl.pallas_call(
        functools.partial(kernel, owners),
        out_shape=(
            jax.ShapeDtypeStruct((1, rows, depth), jnp.float32),
            jax.ShapeDtypeStruct((1, images, width), jnp.float32),
        ),
        in_specs=[scalar, scalar, vmem, anywhere, anywhere, anywhere],
        out_specs=(anywhere, vmem),
        scratch_shapes=[
            pltpu.VMEM((rows, width), jnp.bfloat16),
            pltpu.VMEM((rows, depth), jnp.bfloat16),
            pltpu.VMEM((depth, width), jnp.bfloat16),
            pltpu.VMEM((POOL_DEVS * rows, width), jnp.bfloat16),
            pltpu.VMEM((POOL_DEVS * rows, width), jnp.bfloat16),
            pltpu.VMEM((rows, width), jnp.float32),
            pltpu.VMEM((rows, width), jnp.bfloat16),
            pltpu.VMEM((rows, depth), jnp.float32),
            pltpu.VMEM((owners, images, width), jnp.bfloat16),
            pltpu.VMEM((owners, images, width), jnp.bfloat16),
            dma((3,)),
            dma,
            dma((COPIES,)),
            dma((COPIES,)),
            dma((COPIES,)),
            dma((COPIES,)),
            dma((owners,)),
            dma((owners,)),
        ],
        compiler_params=pltpu.CompilerParams(
            collective_id=0, has_side_effects=True, vmem_limit_bytes=48 * 1024 * 1024
        ),
    )(
        logit_scale.reshape((1,)),
        logit_bias.reshape((1,)),
        image_of_pair,
        image_raw,
        text_feat,
        text_head,
    )


def solution(mesh):
    placed = (P("dp", "loop", None), P("dp", "loop", None), P(), P("dp", "loop"), P(), P())
    return jax.shard_map(
        functools.partial(shards, mesh.shape["dp"]),
        mesh=mesh,
        in_specs=placed,
        out_specs=(P("dp", "loop", None), P("loop", "dp", None)),
        check_vma=False,
    )
```

time: 142 us -> 43.4 us (0.31)
  waiting for transfers between devices: 86.4 us -> 0 us
  Pallas kernels: 0 us -> 35.1 us
  matrix products: 29.3 us -> 0 us
  other arithmetic: 10.3 us -> 0 us
  starting transfers between devices: 9.89 us -> 0 us
  local copies, waits for them, and re-layouts: 3.45 us -> 5.85 us
    ppermute x3 -> x0, waiting for transfers between devices: 73.4 us -> none  [from_partner(): return lax.ppermute(value, axis, pairs)]
    pallas_call x0 -> x1, Pallas kernels: none -> 35.1 us  [shards(): pl.pallas_call(functools.partial(kernel, owners), out_shape=(jax.ShapeDty...]
    dot_general x12 -> x0, matrix products: 29.3 us -> none  [the longest x4 11.5 us: left_product(): lax.dot_general(weight, block, (((0,), (0,)), ((), ())), preferred_elemen...]
    all_to_all x1 -> x0, waiting for transfers between devices: 13 us -> none  [shards(): lax.all_to_all(table, 'dp', split_axis=0, concat_axis=0, tiled=True)]
    select_n x2 -> x0, other arithmetic: 6.88 us -> none  [shards(): jnp.where(lower, jnp.concatenate([held, far], axis=1), jnp.concatenate([f...]
    ppermute x3 -> x0, starting transfers between devices: 5.08 us -> none  [from_partner(): return lax.ppermute(value, axis, pairs)]
    all_to_all x1 -> x0, starting transfers between devices: 4.81 us -> none  [shards(): lax.all_to_all(table, 'dp', split_axis=0, concat_axis=0, tiled=True)]
    unnamed x16 -> x10, local copies, waits for them, and re-layouts: 3.45 us -> 5.85 us
  transfers between devices with their start and end apart: 4 -> 0, of which waited for: 4 -> 0; matrix products, arithmetic and copies ran while one was open for 13% -> 0% of each run, Pallas kernels for 0% -> 0%
where the time goes in v1:
time: 43.4 us; the launch traced here: 42.9 us
  Pallas kernels  35.1 us (81%)
  local copies, waits for them, and re-layouts  5.85 us (13%)
  between operations  1.94 us (4%)
    pallas_call x1, Pallas kernels, shards(): pl.pallas_call(functools.partial(kernel, owners), out_shape=(jax.ShapeDty...  35.1 us
    unnamed x10, local copies, waits for them, and re-layouts  5.85 us

profile of v1, /device:TPU:0, one launch (start us, length us, event | category | flops | bytes accessed | tf_op | source)
XLA Modules:
  0.0 42.9 jit_solution(5998995924604444376)
XLA Ops:
  1.9 0.0 copy-start
  1.9 1.7 %copy-done = bf16[1152,1152]{1,0:T(8,128)(2,1)S(1)} copy-done((bf16[1152,1152]{1,0:T(8,128)(2,1)S(1)}, bf16[1152,1152]{1,0:T(8,128)(2,1)}, u32[]{:S(2)}) %copy-start) | copy-done | bytes 2654232
  3.7 0.0 copy-start.1
  3.7 1.0 %copy-done.1 = bf16[1,128,1152]{2,1,0:T(8,128)(2,1)S(1)} copy-done((bf16[1,128,1152]{2,1,0:T(8,128)(2,1)S(1)}, bf16[1,128,1152]{2,1,0:T(8,128)(2,1)}, u32[]{:S(2)}) %copy-start.1) | copy-done | bytes 294936
  4.6 0.0 copy-start.2
  4.6 1.0 %copy-done.2 = bf16[1,128,1152]{2,1,0:T(8,128)(2,1)S(1)} copy-done((bf16[1,128,1152]{2,1,0:T(8,128)(2,1)S(1)}, bf16[1,128,1152]{2,1,0:T(8,128)(2,1)}, u32[]{:S(2)}) %copy-start.2) | copy-done | bytes 294936
  5.6 0.0 copy-start.3
  5.6 0.7 %copy-done.3 = s32[1,128]{1,0:T(1,128)S(1)} copy-done((s32[1,128]{1,0:T(1,128)S(1)}, s32[1,128]{1,0:T(1,128)}, u32[]{:S(2)}) %copy-start.3) | copy-done | bytes 536
  6.3 35.1 %shard_map.77 = (f32[1,128,1152]{2,1,0:T(8,128)S(1)}, f32[1,64,1152]{2,1,0:T(8,128)S(1)}) custom-call(f32[1]{0:T(128)} %bitcast.2.scale_ref, f32[1]{0:T(128)} %bitcast.3.shift_ref, s32[1,128]{1,0:T(1,128)S(1)} %copy-done.3, bf16[1,128,1152]{2,1,0:T(8,128)(2,1)S(1)} %copy-done.1, bf16[1,128,1152]{2,1,0:T(8,128)(2,1)S(1)} %copy-done.2, ...), custom_call_target="tpu_custom_call" | custom-call | tf_op jit(solution)/shard_map/pallas_call | solution.py:257
  41.4 0.8 %copy.12 = f32[1,128,1152]{2,1,0:T(8,128)} copy(f32[1,128,1152]{2,1,0:T(8,128)S(1)} %get-tuple-element.4) | data formatting | bytes 1179648
  42.2 0.7 %copy.13 = f32[1,64,1152]{2,1,0:T(8,128)} copy(f32[1,64,1152]{2,1,0:T(8,128)S(1)} %get-tuple-element.5) | data formatting | bytes 589824
Async XLA Ops:
  1.9 1.8 %copy-start = (bf16[1152,1152]{1,0:T(8,128)(2,1)S(1)}, bf16[1152,1152]{1,0:T(8,128)(2,1)}, u32[]{:S(2)}) copy-start(bf16[1152,1152]{1,0:T(8,128)(2,1)} %head_ref.1) | copy-start | bytes 7962628
  3.7 1.0 %copy-start.1 = (bf16[1,128,1152]{2,1,0:T(8,128)(2,1)S(1)}, bf16[1,128,1152]{2,1,0:T(8,128)(2,1)}, u32[]{:S(2)}) copy-start(bf16[1,128,1152]{2,1,0:T(8,128)(2,1)} %image_ref.1) | copy-start | bytes 884740
  4.6 1.0 %copy-start.2 = (bf16[1,128,1152]{2,1,0:T(8,128)(2,1)S(1)}, bf16[1,128,1152]{2,1,0:T(8,128)(2,1)}, u32[]{:S(2)}) copy-start(bf16[1,128,1152]{2,1,0:T(8,128)(2,1)} %feat_ref.1) | copy-start | bytes 884740
  5.6 0.7 %copy-start.3 = (s32[1,128]{1,0:T(1,128)S(1)}, s32[1,128]{1,0:T(1,128)}, u32[]{:S(2)}) copy-start(s32[1,128]{1,0:T(1,128)} %label_ref.1) | copy-start | bytes 1540

commit v2 on v1

v2 whole, which is shorter than its diff:
```python
import functools

import jax
import jax.numpy as jnp
from jax import lax
from jax.experimental import pallas as pl
from jax.experimental.pallas import tpu as pltpu
from jax.sharding import PartitionSpec as P

EPS = 1e-06
POOL_DEVS = 8
CORE, NEAR, FAR = 1, 2, 4
NT = (((1,), (1,)), ((), ()))


def partner(me, mask):
    bit = lax.rem(lax.div(me, mask), 2)
    return me + mask * (1 - 2 * bit)


class Spread:
    def __init__(self, buf, send, recv, me, rows):
        half = rows // 2
        peers = {m: partner(me, m) for m in (CORE, NEAR, FAR)}

        def copy(at, slot, mask, first, count):
            source = buf.at[pl.ds(slot * rows + first, count)]
            target = buf.at[pl.ds((slot ^ mask) * rows + first, count)]
            return pltpu.make_async_remote_copy(
                src_ref=source,
                dst_ref=target,
                send_sem=send.at[at],
                recv_sem=recv.at[at],
                device_id={"loop": peers[mask]},
                device_id_type=pl.DeviceIdType.MESH,
            )

        self.own_core = copy(0, 0, CORE, 0, rows)
        self.near_a = copy(1, 0, NEAR, 0, half)
        self.near_b = copy(2, 0, NEAR, half, half)
        self.far_a = copy(3, 0, FAR, 0, half)
        self.far_b = copy(4, 0, FAR, half, half)
        self.near_core = copy(5, NEAR, CORE, 0, rows)
        self.far_core = copy(6, FAR, CORE, 0, rows)
        piece = half // 2
        self.diag_a = [copy(7 + i, NEAR, FAR, i * piece, piece) for i in range(2)]
        self.diag_b = [copy(9 + i, FAR, NEAR, half + i * piece, piece) for i in range(2)]
        diag = NEAR | FAR
        self.diag_core_a = [copy(11 + i, diag, CORE, i * piece, piece) for i in range(2)]
        self.diag_core_b = [copy(13 + i, diag, CORE, half + i * piece, piece) for i in range(2)]

    def forward(self):
        self.near_a.wait_recv()
        for c in self.diag_a:
            c.start()
        self.far_b.wait_recv()
        for c in self.diag_b:
            c.start()

    def relay_diag(self):
        for i in range(2):
            self.diag_a[i].wait_recv()
            self.diag_core_a[i].start()
            self.diag_b[i].wait_recv()
            self.diag_core_b[i].start()

    def await_diag_core(self):
        for c in self.diag_core_a + self.diag_core_b:
            c.wait_recv()

    def drain(self, diag):
        for c in (self.own_core, self.near_a, self.near_b, self.far_a, self.far_b, self.near_core, self.far_core):
            c.wait_send()
        for c in self.diag_core_a + self.diag_core_b:
            c.wait_send()
        if diag:
            self.drain_diag()

    def drain_diag(self):
        for c in self.diag_a + self.diag_b:
            c.wait_send()


COPIES = 15


class Line:
    def __init__(self, refs, owner, label_row, width, piece_ends):
        self.label_out, self.label_in, self.pair_in, self.table_out, self.table_in, self.own, send, recv = refs
        self.label_row = label_row
        self.images = self.table_out.shape[1]
        self.pieces = piece_ends
        count = len(piece_ends)
        self.is_end = owner * (3 - owner) == 0
        self.is_inner = owner * (3 - owner) != 0
        inner = 1 + lax.div(owner, 3)
        end = (owner - 1) * 3
        self.owner, self.end, self.far_inner, self.far_end = owner, end, 3 - owner, 3 - end

        def copy(at, source, target, device):
            return pltpu.make_async_remote_copy(
                src_ref=source,
                dst_ref=target,
                send_sem=send.at[at],
                recv_sem=recv.at[at],
                device_id={"dp": device},
                device_id_type=pl.DeviceIdType.MESH,
            )

        self.labels = copy(0, self.label_out, self.label_in, inner)
        self.copy = copy
        self.count = count
        self.inner = inner
        self.to_end = copy(1, self.table_out.at[0], self.table_in.at[0], end)

    def rows_copy(self, pair_v, k):
        first, size = self.pieces[k]
        part = (slice(None), pl.ds(first, size))
        return self.copy(2 + k, pair_v.at[part], self.pair_in.at[part], self.inner)

    def across_copy(self, slot, k):
        first, size = self.pieces[k]
        part = (slot, slice(None), pl.ds(first, size))
        device = self.far_inner if slot == 1 else self.far_end
        at = 2 + slot * self.count + k
        return self.copy(at, self.table_out.at[part], self.table_in.at[part], device)

    def onehot(self, label_row, device):
        rows = label_row.shape[1]
        ids = lax.broadcasted_iota(jnp.int32, (self.images, rows), 0) + device * self.images
        return jnp.where(ids.astype(jnp.float32) == label_row, 1.0, 0.0).astype(jnp.bfloat16)

    def tables(self, label_row, devices, values):
        hot = jnp.concatenate([self.onehot(label_row, d) for d in devices], axis=0)
        return jnp.dot(hot, values, preferred_element_type=jnp.float32)

    def send_labels(self):
        @pl.when(self.is_end)
        def _():
            self.labels.start()

    def first(self, pair_v, d_image_ref):
        images = self.images

        @pl.when(self.is_end)
        def _():
            for k in range(self.count):
                self.rows_copy(pair_v, k).start()
            d_image_ref[0] = self.tables(self.label_row, [self.owner], pair_v[...])

        @pl.when(self.is_inner)
        def _():
            self.table_out[0] = self.tables(self.label_row, [self.end], pair_v[...]).astype(jnp.bfloat16)
            self.to_end.start()
            devices = [self.far_inner, self.far_end, self.owner]
            self.own[...] = self.tables(self.label_row, devices, pair_v[...])
            self.labels.wait_recv()

    def step(self, pair_v, k, d_image_ref):
        first, size = self.pieces[k]
        images = self.images

        @pl.when(self.is_inner)
        def _():
            self.rows_copy(pair_v, k).wait_recv()
            part = pl.ds(first, size)
            devices = [self.far_inner, self.far_end, self.owner]
            there = self.label_in[pl.ds(0, 1)]
            sums = self.own[:, part] + self.tables(there, devices, self.pair_in[:, part])
            for slot in (1, 2):
                rows = sums[(slot - 1) * images : slot * images]
                self.table_out[slot, :, part] = rows.astype(jnp.bfloat16)
                self.across_copy(slot, k).start()
            d_image_ref[0, :, part] = sums[2 * images :]

    def last(self, pair_v, d_image_ref):
        @pl.when(self.is_end)
        def _():
            self.to_end.wait_recv()
            for k, (first, size) in enumerate(self.pieces):
                part = pl.ds(first, size)
                self.across_copy(2, k).wait_recv()
                d_image_ref[0, :, part] += (
                    self.table_in[0, :, part].astype(jnp.float32) + self.table_in[2, :, part].astype(jnp.float32)
                )
            self.labels.wait_send()
            for k in range(self.count):
                self.rows_copy(pair_v, k).wait_send()

        @pl.when(self.is_inner)
        def _():
            for k, (first, size) in enumerate(self.pieces):
                part = pl.ds(first, size)
                self.across_copy(1, k).wait_recv()
                d_image_ref[0, :, part] += self.table_in[1, :, part].astype(jnp.float32)
            self.to_end.wait_send()
            for k in range(self.count):
                self.across_copy(1, k).wait_send()
                self.across_copy(2, k).wait_send()


class Direct:
    def __init__(self, refs, owner, label_row, owners):
        self.table_out, self.table_in, self.send, self.recv = refs
        self.owner, self.label_row, self.owners = owner, label_row, owners

    def copy(self, apart):
        return pltpu.make_async_remote_copy(
            src_ref=self.table_out.at[apart],
            dst_ref=self.table_in.at[apart],
            send_sem=self.send.at[apart],
            recv_sem=self.recv.at[apart],
            device_id={"dp": lax.rem(self.owner + apart, self.owners)},
            device_id_type=pl.DeviceIdType.MESH,
        )

    def table(self, pair_v, apart):
        images, rows = self.table_out.shape[1], self.label_row.shape[1]
        first = lax.rem(self.owner + apart, self.owners) * images
        ids = lax.broadcasted_iota(jnp.int32, (images, rows), 0) + first
        onehot = jnp.where(ids.astype(jnp.float32) == self.label_row, 1.0, 0.0).astype(jnp.bfloat16)
        return jnp.dot(onehot, pair_v[...], preferred_element_type=jnp.float32)

    def send_labels(self):
        pass

    def first(self, pair_v, d_image_ref):
        for apart in range(1, self.owners):
            self.table_out[apart] = self.table(pair_v, apart).astype(jnp.bfloat16)
            self.copy(apart).start()
        d_image_ref[0] = self.table(pair_v, 0)

    def step(self, pair_v, k, d_image_ref):
        pass

    def last(self, pair_v, d_image_ref):
        for apart in range(1, self.owners):
            self.copy(apart).wait_recv()
            d_image_ref[0] += self.table_in[apart].astype(jnp.float32)
        for apart in range(1, self.owners):
            self.copy(apart).wait_send()


def pieces_of(width):
    lanes = width // 128
    small = max(lanes // 4, 1)
    sizes = [lanes - 3 * small] + [small] * 3 if lanes > 3 * small else [lanes]
    starts = [sum(sizes[:i]) for i in range(len(sizes))]
    return [(128 * a, 128 * b) for a, b in zip(starts, sizes)]


def kernel(
    owners,
    scale_ref,
    shift_ref,
    label_ref,
    image_ref,
    feat_ref,
    head_ref,
    d_feat_ref,
    d_image_ref,
    image_v,
    feat_v,
    head_v,
    xbuf,
    ybuf,
    unit_y_v,
    d_pair_v,
    load_sem,
    x_send,
    x_recv,
    y_send,
    y_recv,
    *dp_refs,
):
    rows, width = image_v.shape
    me = lax.axis_index("loop")
    owner = lax.axis_index("dp")

    load_image = pltpu.make_async_copy(image_ref.at[0], image_v, load_sem.at[0])
    load_feat = pltpu.make_async_copy(feat_ref.at[0], feat_v, load_sem.at[1])
    load_head = pltpu.make_async_copy(head_ref, head_v, load_sem.at[2])
    load_image.start()
    load_feat.start()
    load_head.start()

    barrier = pltpu.get_barrier_semaphore()
    for mask in (CORE, NEAR, FAR):
        pl.semaphore_signal(
            barrier, inc=1, device_id={"loop": partner(me, mask)}, device_id_type=pl.DeviceIdType.MESH
        )
    for apart in range(1, owners):
        pl.semaphore_signal(
            barrier,
            inc=1,
            device_id={"dp": lax.rem(owner + apart, owners)},
            device_id_type=pl.DeviceIdType.MESH,
        )

    scale = scale_ref[0]
    shift = shift_ref[0]
    label_row = label_ref[...].astype(jnp.float32)
    label_grid = jnp.broadcast_to(label_row, (rows, rows))
    same = label_grid == label_grid.T

    xs = Spread(xbuf, x_send, x_recv, me, rows)
    ys = Spread(ybuf, y_send, y_recv, me, rows)
    pieces = pieces_of(width)
    if owners == 4:
        sums = Line(dp_refs, owner, label_row, width, pieces)
        sums.label_out[...] = jnp.broadcast_to(label_row, sums.label_out.shape)
    else:
        sums = Direct(dp_refs, owner, label_row, owners)

    load_image.wait()
    image = image_v[...].astype(jnp.float32)
    inv_x = lax.rsqrt(jnp.sum(image * image, axis=-1, keepdims=True) + EPS)
    xbuf[pl.ds(0, rows)] = (image * inv_x).astype(jnp.bfloat16)

    pl.semaphore_wait(barrier, 3 + owners - 1)
    xs.near_a.start()
    xs.far_b.start()
    xs.own_core.start()
    sums.send_labels()

    load_feat.wait()
    load_head.wait()
    text_pre = jnp.dot(feat_v[...], head_v[...], preferred_element_type=jnp.float32)
    inv_y = lax.rsqrt(jnp.sum(text_pre * text_pre, axis=-1, keepdims=True) + EPS)
    unit_y = text_pre * inv_y
    ybuf[pl.ds(0, rows)] = unit_y.astype(jnp.bfloat16)
    ys.near_a.start()
    ys.far_b.start()
    ys.near_b.start()
    ys.far_a.start()
    ys.own_core.start()
    unit_y_v[...] = unit_y

    def part(mine, buf, slot, count):
        block = buf[pl.ds(slot * rows, count * rows)]
        logits = scale * lax.dot_general(mine, block, NT, preferred_element_type=jnp.float32) + shift
        if slot == 0:
            flip = jnp.concatenate([same, jnp.zeros_like(same)], axis=1)
            value = jax.nn.sigmoid(jnp.where(flip, -logits, logits))
            value = jnp.where(flip, -value, value)
        else:
            value = jax.nn.sigmoid(logits)
        return jnp.dot(value.astype(jnp.bfloat16), block, preferred_element_type=jnp.float32)

    x_own = xbuf[pl.ds(0, rows)]
    y_own = ybuf[pl.ds(0, rows)]

    ys.own_core.wait_recv()
    total = part(x_own, ybuf, 0, 2)
    ys.forward()
    ys.near_b.wait_recv()
    ys.near_core.start()
    ys.far_a.wait_recv()
    ys.far_core.start()
    ys.drain_diag()
    xs.near_b.start()
    xs.far_a.start()
    xs.forward()
    ys.near_core.wait_recv()
    total = total + part(x_own, ybuf, 2, 2)
    ys.far_core.wait_recv()
    total = total + part(x_own, ybuf, 4, 2)
    ys.relay_diag()
    total = total + part(x_own, ybuf, 6, 1)
    ys.await_diag_core()
    total = total + part(x_own, ybuf, 7, 1)
    grad = scale * total
    unit_x = image * inv_x
    d_pair = (grad - unit_x * jnp.sum(unit_x * grad, axis=-1, keepdims=True)) * inv_x
    d_pair_v[...] = d_pair.astype(jnp.bfloat16)

    sums.first(d_pair_v, d_image_ref)
    xs.near_b.wait_recv()
    xs.near_core.start()
    xs.far_a.wait_recv()
    xs.far_core.start()
    xs.own_core.wait_recv()
    total = part(y_own, xbuf, 0, 2)
    sums.step(d_pair_v, 0, d_image_ref)
    xs.near_core.wait_recv()
    total = total + part(y_own, xbuf, 2, 2)
    xs.far_core.wait_recv()
    total = total + part(y_own, xbuf, 4, 2)
    sums.step(d_pair_v, 1, d_image_ref)
    xs.relay_diag()
    total = total + part(y_own, xbuf, 6, 1)
    sums.step(d_pair_v, 2, d_image_ref)
    xs.await_diag_core()
    total = total + part(y_own, xbuf, 7, 1)
    sums.step(d_pair_v, 3, d_image_ref)
    grad = scale * total
    unit_y = unit_y_v[...]
    d_text = (grad - unit_y * jnp.sum(unit_y * grad, axis=-1, keepdims=True)) * inv_y
    d_feat_ref[0] = lax.dot_general(
        d_text.astype(jnp.bfloat16), head_v[...], NT, preferred_element_type=jnp.float32
    )

    sums.last(d_pair_v, d_image_ref)
    xs.drain(True)
    ys.drain(False)


def shards(owners, image_raw, text_feat, text_head, image_of_pair, logit_scale, logit_bias):
    _, rows, width = image_raw.shape
    depth = text_head.shape[0]
    images = rows // 2
    hbm = pl.BlockSpec(memory_space=pltpu.HBM)
    scalar = pl.BlockSpec(memory_space=pltpu.SMEM)
    vmem = pl.BlockSpec(memory_space=pltpu.VMEM)
    dma = pltpu.SemaphoreType.DMA
    if owners == 4:
        copies = 2 + 3 * len(pieces_of(width))
        dp_scratch = [
            pltpu.VMEM((8, rows), jnp.float32),
            pltpu.VMEM((8, rows), jnp.float32),
            pltpu.VMEM((rows, width), jnp.bfloat16),
            pltpu.VMEM((3, images, width), jnp.bfloat16),
            pltpu.VMEM((3, images, width), jnp.bfloat16),
            pltpu.VMEM((3 * images, width), jnp.float32),
            dma((copies,)),
            dma((copies,)),
        ]
    else:
        dp_scratch = [
            pltpu.VMEM((owners, images, width), jnp.bfloat16),
            pltpu.VMEM((owners, images, width), jnp.bfloat16),
            dma((owners,)),
            dma((owners,)),
        ]
    return pl.pallas_call(
        functools.partial(kernel, owners),
        out_shape=(
            jax.ShapeDtypeStruct((1, rows, depth), jnp.float32),
            jax.ShapeDtypeStruct((1, images, width), jnp.float32),
        ),
        in_specs=[scalar, scalar, vmem, hbm, hbm, hbm],
        out_specs=(vmem, vmem),
        scratch_shapes=[
            pltpu.VMEM((rows, width), jnp.bfloat16),
            pltpu.VMEM((rows, depth), jnp.bfloat16),
            pltpu.VMEM((depth, width), jnp.bfloat16),
            pltpu.VMEM((POOL_DEVS * rows, width), jnp.bfloat16),
            pltpu.VMEM((POOL_DEVS * rows, width), jnp.bfloat16),
            pltpu.VMEM((rows, width), jnp.float32),
            pltpu.VMEM((rows, width), jnp.bfloat16),
            dma((3,)),
            dma((COPIES,)),
            dma((COPIES,)),
            dma((COPIES,)),
            dma((COPIES,)),
            *dp_scratch,
        ],
        compiler_params=pltpu.CompilerParams(
            collective_id=0, has_side_effects=True, vmem_limit_bytes=56 * 1024 * 1024
        ),
    )(
        logit_scale.reshape((1,)),
        logit_bias.reshape((1,)),
        image_of_pair,
        image_raw,
        text_feat,
        text_head,
    )


def solution(mesh):
    placed = (P("dp", "loop", None), P("dp", "loop", None), P(), P("dp", "loop"), P(), P())
    return jax.shard_map(
        functools.partial(shards, mesh.shape["dp"]),
        mesh=mesh,
        in_specs=placed,
        out_specs=(P("dp", "loop", None), P("loop", "dp", None)),
        check_vma=False,
    )
```

time: 43.4 us -> 42.7 us (0.984)
  local copies, waits for them, and re-layouts: 5.85 us -> 3.61 us
  Pallas kernels: 35.1 us -> 37 us
    unnamed x10 -> x2, local copies, waits for them, and re-layouts: 5.85 us -> 3.61 us
    pallas_call x1, Pallas kernels: 35.1 us -> 37 us  [shards(): pl.pallas_call(functools.partial(kernel, owners), out_shape=(jax.ShapeDty...]
where the time goes in v2:
time: 42.7 us; the launch traced here: 42.5 us
  Pallas kernels  37 us (87%)
  local copies, waits for them, and re-layouts  3.61 us (8%)
  between operations  1.93 us (5%)
    pallas_call x1, Pallas kernels, shards(): pl.pallas_call(functools.partial(kernel, owners), out_shape=(jax.ShapeDty...  37 us
    unnamed x2, local copies, waits for them, and re-layouts  3.61 us

profile of v2, /device:TPU:0, one launch (start us, length us, event | category | flops | bytes accessed | tf_op | source)
XLA Modules:
  0.0 42.5 jit_solution(15085265642701436478)
XLA Ops:
  1.9 37.0 %shard_map.77 = (f32[1,128,1152]{2,1,0:T(8,128)}, f32[1,64,1152]{2,1,0:T(8,128)}) custom-call(f32[1]{0:T(128)} %bitcast.2.scale_ref, f32[1]{0:T(128)} %bitcast.3.shift_ref, s32[1,128]{1,0:T(1,128)} %label_ref.1, bf16[1,128,1152]{2,1,0:T(8,128)(2,1)} %image_ref.1, bf16[1,128,1152]{2,1,0:T(8,128)(2,1)} %feat_ref.1, bf16[1152,1152]{1,0:T(8,128)(2,1)} %head_ref.1), custom_call_target="tpu_custom_call" | custom-call | tf_op jit(solution)/shard_map/pallas_call | solution.py:435
  38.9 1.9 %copy.12 = f32[1,128,1152]{2,1,0:T(8,128)} copy(f32[1,128,1152]{2,1,0:T(8,128)} %get-tuple-element.4) | data formatting | bytes 1179648
  40.8 1.7 %copy.13 = f32[1,64,1152]{2,1,0:T(8,128)} copy(f32[1,64,1152]{2,1,0:T(8,128)} %get-tuple-element.5) | data formatting | bytes 589824

commit v3 on v2

v3 whole, which is shorter than its diff:
```python
import functools

import jax
import jax.numpy as jnp
from jax import lax
from jax.experimental import pallas as pl
from jax.experimental.pallas import tpu as pltpu
from jax.sharding import PartitionSpec as P

EPS = 1e-06
CORE, NEAR, FAR = 1, 2, 4
NT = (((1,), (1,)), ((), ()))


def partner(me, mask):
    bit = lax.rem(lax.div(me, mask), 2)
    return me + mask * (1 - 2 * bit)


class Spread:
    def __init__(self, buf, send, recv, me, rows, mask):
        def copy(at, source, target, device, first, count):
            return pltpu.make_async_remote_copy(
                src_ref=buf.at[pl.ds(source * rows + first, count)],
                dst_ref=buf.at[pl.ds(target * rows + first, count)],
                send_sem=send.at[at],
                recv_sem=recv.at[at],
                device_id={"loop": device},
                device_id_type=pl.DeviceIdType.MESH,
            )

        core, side = partner(me, CORE), partner(me, mask)
        piece = rows // STEPS
        self.own_core = copy(0, 0, 2, core, 0, rows)
        self.direct = [copy(1 + i, 0, 1, side, i * piece, piece) for i in range(STEPS)]
        self.relay = [copy(1 + STEPS + i, 1, 3, core, i * piece, piece) for i in range(STEPS)]

    def start(self):
        for c in self.direct:
            c.start()
        self.own_core.start()

    def hand_on(self, i):
        self.direct[i].wait_recv()
        self.relay[i].start()

    def drain(self):
        for c in [self.own_core] + self.direct + self.relay:
            c.wait_send()


STEPS = 4
COPIES = 1 + 2 * STEPS


class Line:
    def __init__(self, refs, owner, label_row, pieces):
        self.label_out, self.label_in, self.pair_in, self.table_out, self.table_in, self.send, self.recv = refs
        self.label_row = label_row
        self.images = self.table_out.shape[1]
        self.pieces = pieces
        self.count = len(pieces)
        self.is_end = owner * (3 - owner) == 0
        self.is_inner = owner * (3 - owner) != 0
        self.inner = 1 + lax.div(owner, 3)
        self.end = (owner - 1) * 3
        self.owner, self.far_inner, self.far_end = owner, 3 - owner, 3 - self.end
        self.label_out[...] = jnp.broadcast_to(label_row, self.label_out.shape)
        self.labels = self.copy(0, self.label_out, self.label_in, self.inner)

    def copy(self, at, source, target, device):
        return pltpu.make_async_remote_copy(
            src_ref=source,
            dst_ref=target,
            send_sem=self.send.at[at],
            recv_sem=self.recv.at[at],
            device_id={"dp": device},
            device_id_type=pl.DeviceIdType.MESH,
        )

    def rows_copy(self, pair_v, k):
        part = (slice(None), pl.ds(*self.pieces[k]))
        return self.copy(1 + k, pair_v.at[part], self.pair_in.at[part], self.inner)

    def table_copy(self, slot, k):
        part = (slot, slice(None), pl.ds(*self.pieces[k]))
        device = (self.end, self.far_inner, self.far_end)[slot]
        at = 1 + (1 + slot) * self.count + k
        return self.copy(at, self.table_out.at[part], self.table_in.at[part], device)

    def tables(self, label_row, devices, values):
        rows = label_row.shape[1]
        ids = lax.broadcasted_iota(jnp.int32, (self.images, rows), 0).astype(jnp.float32)
        firsts = [(d * self.images).astype(jnp.float32) for d in devices]
        hot = jnp.concatenate([jnp.where(ids + f == label_row, 1.0, 0.0) for f in firsts], axis=0)
        return jnp.dot(hot.astype(jnp.bfloat16), values, preferred_element_type=jnp.float32)

    def send_labels(self):
        @pl.when(self.is_end)
        def _():
            self.labels.start()

    def ready(self, pair_v, k, d_image_ref):
        part = pl.ds(*self.pieces[k])

        @pl.when(self.is_end)
        def _():
            self.rows_copy(pair_v, k).start()
            d_image_ref[0, :, part] = self.tables(self.label_row, [self.owner], pair_v[:, part])

        @pl.when(self.is_inner)
        def _():
            self.table_out[0, :, part] = self.tables(self.label_row, [self.end], pair_v[:, part]).astype(jnp.bfloat16)
            self.table_copy(0, k).start()
            if k == 0:
                self.labels.wait_recv()

    def step(self, pair_v, k, d_image_ref):
        images = self.images
        part = pl.ds(*self.pieces[k])

        @pl.when(self.is_inner)
        def _():
            devices = [self.far_inner, self.far_end, self.owner]
            sums = self.tables(self.label_row, devices, pair_v[:, part])
            self.rows_copy(pair_v, k).wait_recv()
            sums = sums + self.tables(self.label_in[pl.ds(0, 1)], devices, self.pair_in[:, part])
            for slot in (1, 2):
                self.table_out[slot, :, part] = sums[(slot - 1) * images : slot * images].astype(jnp.bfloat16)
                self.table_copy(slot, k).start()
            d_image_ref[0, :, part] = sums[2 * images :]

    def last(self, pair_v, d_image_ref):
        @pl.when(self.is_end)
        def _():
            for k, piece in enumerate(self.pieces):
                part = pl.ds(*piece)
                self.table_copy(0, k).wait_recv()
                self.table_copy(2, k).wait_recv()
                d_image_ref[0, :, part] += (
                    self.table_in[0, :, part].astype(jnp.float32) + self.table_in[2, :, part].astype(jnp.float32)
                )
            self.labels.wait_send()
            for k in range(self.count):
                self.rows_copy(pair_v, k).wait_send()

        @pl.when(self.is_inner)
        def _():
            for k, piece in enumerate(self.pieces):
                part = pl.ds(*piece)
                self.table_copy(1, k).wait_recv()
                d_image_ref[0, :, part] += self.table_in[1, :, part].astype(jnp.float32)
            for k in range(self.count):
                for slot in range(3):
                    self.table_copy(slot, k).wait_send()


class Direct:
    def __init__(self, refs, owner, label_row, owners):
        self.table_out, self.table_in, self.send, self.recv = refs
        self.owner, self.label_row, self.owners = owner, label_row, owners

    def copy(self, apart):
        return pltpu.make_async_remote_copy(
            src_ref=self.table_out.at[apart],
            dst_ref=self.table_in.at[apart],
            send_sem=self.send.at[apart],
            recv_sem=self.recv.at[apart],
            device_id={"dp": lax.rem(self.owner + apart, self.owners)},
            device_id_type=pl.DeviceIdType.MESH,
        )

    def table(self, pair_v, apart):
        images, rows = self.table_out.shape[1], self.label_row.shape[1]
        first = lax.rem(self.owner + apart, self.owners) * images
        ids = lax.broadcasted_iota(jnp.int32, (images, rows), 0) + first
        onehot = jnp.where(ids.astype(jnp.float32) == self.label_row, 1.0, 0.0).astype(jnp.bfloat16)
        return jnp.dot(onehot, pair_v[...], preferred_element_type=jnp.float32)

    def send_labels(self):
        pass

    def ready(self, pair_v, k, d_image_ref):
        if k + 1 < len(pieces_of(pair_v.shape[1])):
            return
        for apart in range(1, self.owners):
            self.table_out[apart] = self.table(pair_v, apart).astype(jnp.bfloat16)
            self.copy(apart).start()
        d_image_ref[0] = self.table(pair_v, 0)

    def step(self, pair_v, k, d_image_ref):
        pass

    def last(self, pair_v, d_image_ref):
        for apart in range(1, self.owners):
            self.copy(apart).wait_recv()
            d_image_ref[0] += self.table_in[apart].astype(jnp.float32)
        for apart in range(1, self.owners):
            self.copy(apart).wait_send()


def pieces_of(width):
    lanes = width // 128
    small = max(lanes // 4, 1)
    sizes = [lanes - 3 * small] + [small] * 3 if lanes > 3 * small else [lanes]
    starts = [sum(sizes[:i]) for i in range(len(sizes))]
    return [(128 * a, 128 * b) for a, b in zip(starts, sizes)]


def kernel(
    owners,
    scale_ref,
    shift_ref,
    label_ref,
    image_ref,
    feat_ref,
    head_ref,
    d_feat_ref,
    d_image_ref,
    label_v,
    image_v,
    feat_v,
    head_v,
    xbuf,
    ybuf,
    x_weight,
    y_weight,
    unit_y_v,
    text_v,
    d_pair_v,
    x_out,
    x_in,
    y_out,
    y_in,
    dots_out,
    dots_in,
    load_sem,
    x_send,
    x_recv,
    y_send,
    y_recv,
    px_send,
    px_recv,
    py_send,
    py_recv,
    *dp_refs,
):
    rows, width = image_v.shape
    me = lax.axis_index("loop")
    owner = lax.axis_index("dp")

    load_image = pltpu.make_async_copy(image_ref.at[0], image_v, load_sem.at[0])
    load_feat = pltpu.make_async_copy(feat_ref.at[0], feat_v, load_sem.at[1])
    load_head = pltpu.make_async_copy(head_ref, head_v, load_sem.at[2])
    load_label = pltpu.make_async_copy(label_ref, label_v, load_sem.at[3])
    load_label.start()
    load_image.start()
    load_feat.start()
    load_head.start()

    barrier = pltpu.get_barrier_semaphore()
    for mask in (CORE, NEAR, FAR):
        pl.semaphore_signal(
            barrier, inc=1, device_id={"loop": partner(me, mask)}, device_id_type=pl.DeviceIdType.MESH
        )
    for apart in range(1, owners):
        pl.semaphore_signal(
            barrier,
            inc=1,
            device_id={"dp": lax.rem(owner + apart, owners)},
            device_id_type=pl.DeviceIdType.MESH,
        )

    scale = scale_ref[0]
    shift = shift_ref[0]
    load_label.wait()
    label_row = label_v[...].astype(jnp.float32)
    label_grid = jnp.broadcast_to(label_row, (rows, rows))
    same = label_grid == label_grid.T

    xs = Spread(xbuf, x_send, x_recv, me, rows, NEAR)
    ys = Spread(ybuf, y_send, y_recv, me, rows, FAR)
    pieces = pieces_of(width)
    if owners == 4:
        sums = Line(dp_refs, owner, label_row, pieces)
    else:
        sums = Direct(dp_refs, owner, label_row, owners)

    def side_copy(source, target, send, recv, at, mask):
        return pltpu.make_async_remote_copy(
            src_ref=source,
            dst_ref=target,
            send_sem=send.at[at],
            recv_sem=recv.at[at],
            device_id={"loop": partner(me, mask)},
            device_id_type=pl.DeviceIdType.MESH,
        )

    columns = [(slice(None), pl.ds(*piece)) for piece in pieces]
    x_parts = [side_copy(x_out.at[c], x_in.at[c], px_send, px_recv, k, NEAR) for k, c in enumerate(columns)]
    y_parts = [side_copy(y_out.at[c], y_in.at[c], py_send, py_recv, k, FAR) for k, c in enumerate(columns)]
    dots_copy = side_copy(dots_out, dots_in, px_send, px_recv, len(pieces), NEAR)

    load_image.wait()
    image = image_v[...].astype(jnp.float32)
    inv_x = lax.rsqrt(jnp.sum(image * image, axis=-1, keepdims=True) + EPS)
    xbuf[pl.ds(0, rows)] = (image * inv_x).astype(jnp.bfloat16)

    pl.semaphore_wait(barrier, 3 + owners - 1)
    xs.start()
    sums.send_labels()

    load_feat.wait()
    load_head.wait()
    text_pre = jnp.dot(feat_v[...], head_v[...], preferred_element_type=jnp.float32)
    inv_y = lax.rsqrt(jnp.sum(text_pre * text_pre, axis=-1, keepdims=True) + EPS)
    unit_y = text_pre * inv_y
    ybuf[pl.ds(0, rows)] = unit_y.astype(jnp.bfloat16)
    ys.start()
    unit_y_v[...] = unit_y

    def weights(mine, first, count, other, block, blocks, weight):
        dots = lax.dot_general(
            mine[pl.ds(first * rows, count * rows)],
            other[pl.ds(block * rows, blocks * rows)],
            NT,
            preferred_element_type=jnp.float32,
        )
        logits = scale * dots + shift
        if first == 0 and block == 0:
            value = jax.nn.sigmoid(jnp.where(same, -logits, logits))
            value = jnp.where(same, -value, value)
        else:
            value = jax.nn.sigmoid(logits)
        value = value.astype(jnp.bfloat16)
        weight[pl.ds(first * rows, count * rows), pl.ds(block * rows, blocks * rows)] = value
        return jnp.sum(value.astype(jnp.float32) * dots, axis=-1, keepdims=True)

    def product(weight, first, buf, column):
        return jnp.dot(weight[pl.ds(first * rows, rows)], buf[column], preferred_element_type=jnp.float32)

    xs.hand_on(0)
    ys.own_core.wait_recv()
    xs.own_core.wait_recv()
    own_dots = weights(xbuf, 0, 1, ybuf, 0, 1, x_weight) + weights(xbuf, 0, 1, ybuf, 2, 1, x_weight)
    weights(ybuf, 0, 1, xbuf, 0, 1, y_weight)
    weights(ybuf, 0, 1, xbuf, 2, 1, y_weight)
    xs.hand_on(1)
    ys.hand_on(0)
    xs.hand_on(2)
    ys.hand_on(1)
    xs.hand_on(3)
    ys.hand_on(2)
    near_dots = weights(xbuf, 1, 1, ybuf, 0, 1, x_weight) + weights(xbuf, 1, 1, ybuf, 2, 1, x_weight)
    ys.hand_on(3)

    near_dots = near_dots + weights(xbuf, 1, 1, ybuf, 1, 1, x_weight)
    for c in ys.relay:
        c.wait_recv()
    near_dots = near_dots + weights(xbuf, 1, 1, ybuf, 3, 1, x_weight)
    dots_out[...] = jnp.broadcast_to(near_dots, (rows, rows)).T[:8]
    dots_copy.start()
    for k, c in enumerate(columns):
        x_out[c] = product(x_weight, 1, ybuf, c).astype(jnp.bfloat16)
        x_parts[k].start()

    for c in xs.relay:
        c.wait_recv()
    weights(ybuf, 1, 1, xbuf, 0, 4, y_weight)
    for k, c in enumerate(columns):
        y_out[c] = product(y_weight, 1, xbuf, c).astype(jnp.bfloat16)
        y_parts[k].start()

    own_dots = own_dots + weights(xbuf, 0, 1, ybuf, 1, 1, x_weight) + weights(xbuf, 0, 1, ybuf, 3, 1, x_weight)
    weights(ybuf, 0, 1, xbuf, 1, 1, y_weight)
    weights(ybuf, 0, 1, xbuf, 3, 1, y_weight)
    for c in columns:
        text_v[c] = product(y_weight, 0, xbuf, c)
    dots_copy.wait_recv()
    there = jnp.broadcast_to(dots_in[pl.ds(0, 1)], (rows, rows)).T[:, :1]
    along = scale * (own_dots + there)
    for k, c in enumerate(columns):
        grad = product(x_weight, 0, ybuf, c)
        unit_x = image_v[c].astype(jnp.float32) * inv_x
        x_parts[k].wait_recv()
        grad = scale * (grad + x_in[c].astype(jnp.float32))
        d_pair_v[c] = ((grad - unit_x * along) * inv_x).astype(jnp.bfloat16)
        sums.ready(d_pair_v, k, d_image_ref)
        if k > 0:
            sums.step(d_pair_v, k - 1, d_image_ref)

    for c in y_parts:
        c.wait_recv()
    grad = scale * (text_v[...] + y_in[...].astype(jnp.float32))
    unit_y = unit_y_v[...]
    d_text = (grad - unit_y * jnp.sum(unit_y * grad, axis=-1, keepdims=True)) * inv_y
    sums.step(d_pair_v, len(pieces) - 1, d_image_ref)
    d_feat_ref[0] = lax.dot_general(
        d_text.astype(jnp.bfloat16), head_v[...], NT, preferred_element_type=jnp.float32
    )

    sums.last(d_pair_v, d_image_ref)
    xs.drain()
    ys.drain()
    for c in x_parts + y_parts + [dots_copy]:
        c.wait_send()


def store(feat_v, image_v, d_feat_ref, d_image_ref, sem):
    feat = pltpu.make_async_copy(feat_v, d_feat_ref, sem.at[0])
    image = pltpu.make_async_copy(image_v, d_image_ref, sem.at[1])
    feat.start()
    image.start()
    feat.wait()
    image.wait()


def shards(owners, image_raw, text_feat, text_head, image_of_pair, logit_scale, logit_bias):
    _, rows, width = image_raw.shape
    depth = text_head.shape[0]
    images = rows // 2
    hbm = pl.BlockSpec(memory_space=pltpu.HBM)
    scalar = pl.BlockSpec(memory_space=pltpu.SMEM)
    vmem = pl.BlockSpec(memory_space=pltpu.VMEM)
    dma = pltpu.SemaphoreType.DMA
    count = len(pieces_of(width))
    if owners == 4:
        dp_scratch = [
            pltpu.VMEM((8, rows), jnp.float32),
            pltpu.VMEM((8, rows), jnp.float32),
            pltpu.VMEM((rows, width), jnp.bfloat16),
            pltpu.VMEM((3, images, width), jnp.bfloat16),
            pltpu.VMEM((3, images, width), jnp.bfloat16),
            dma((1 + 4 * count,)),
            dma((1 + 4 * count,)),
        ]
    else:
        dp_scratch = [
            pltpu.VMEM((owners, images, width), jnp.bfloat16),
            pltpu.VMEM((owners, images, width), jnp.bfloat16),
            dma((owners,)),
            dma((owners,)),
        ]
    results = (
        jax.ShapeDtypeStruct((1, rows, depth), jnp.float32),
        jax.ShapeDtypeStruct((1, images, width), jnp.float32),
    )
    gradients = pl.pallas_call(
        functools.partial(kernel, owners),
        out_shape=results,
        in_specs=[scalar, scalar, hbm, hbm, hbm, hbm],
        out_specs=(vmem, vmem),
        scratch_shapes=[
            pltpu.VMEM((1, rows), jnp.int32),
            pltpu.VMEM((rows, width), jnp.bfloat16),
            pltpu.VMEM((rows, depth), jnp.bfloat16),
            pltpu.VMEM((depth, width), jnp.bfloat16),
            pltpu.VMEM((4 * rows, width), jnp.bfloat16),
            pltpu.VMEM((4 * rows, width), jnp.bfloat16),
            pltpu.VMEM((2 * rows, 4 * rows), jnp.bfloat16),
            pltpu.VMEM((2 * rows, 4 * rows), jnp.bfloat16),
            pltpu.VMEM((rows, width), jnp.float32),
            pltpu.VMEM((rows, width), jnp.float32),
            pltpu.VMEM((rows, width), jnp.bfloat16),
            pltpu.VMEM((rows, width), jnp.bfloat16),
            pltpu.VMEM((rows, width), jnp.bfloat16),
            pltpu.VMEM((rows, width), jnp.bfloat16),
            pltpu.VMEM((rows, width), jnp.bfloat16),
            pltpu.VMEM((8, rows), jnp.float32),
            pltpu.VMEM((8, rows), jnp.float32),
            dma((4,)),
            dma((COPIES,)),
            dma((COPIES,)),
            dma((COPIES,)),
            dma((COPIES,)),
            dma((count + 1,)),
            dma((count + 1,)),
            dma((count,)),
            dma((count,)),
            *dp_scratch,
        ],
        compiler_params=pltpu.CompilerParams(
            collective_id=0, has_side_effects=True, vmem_limit_bytes=32 * 1024 * 1024
        ),
    )(
        logit_scale.reshape((1,)),
        logit_bias.reshape((1,)),
        *(
            pltpu.with_memory_space_constraint(a, pltpu.HBM)
            for a in (image_of_pair, image_raw, text_feat, text_head)
        ),
    )
    return pl.pallas_call(
        store,
        out_shape=results,
        in_specs=[vmem, vmem],
        out_specs=(hbm, hbm),
        scratch_shapes=[dma((2,))],
    )(*gradients)


def solution(mesh):
    placed = (P("dp", "loop", None), P("dp", "loop", None), P(), P("dp", "loop"), P(), P())
    return jax.shard_map(
        functools.partial(shards, mesh.shape["dp"]),
        mesh=mesh,
        in_specs=placed,
        out_specs=(P("dp", "loop", None), P("loop", "dp", None)),
        check_vma=False,
    )
```

time: 42.7 us -> 40.4 us (0.946)
  local copies, waits for them, and re-layouts: 3.61 us -> 1.52 us
    unnamed x2 -> x4, local copies, waits for them, and re-layouts: 3.61 us -> 1.52 us
    pallas_call x1 -> x2, Pallas kernels: 37 us -> 36.7 us  [the longest x1 34.7 us: shards(): pl.pallas_call(functools.partial(kernel, owners), out_shape=results, in_s...]
where the time goes in v3:
time: 40.4 us; the launch traced here: 40.2 us
  Pallas kernels  36.7 us (91%)
  between operations  1.94 us (5%)
  local copies, waits for them, and re-layouts  1.52 us (4%)
    pallas_call x1, Pallas kernels, shards(): pl.pallas_call(functools.partial(kernel, owners), out_shape=results, in_s...  34.7 us
    pallas_call x1, Pallas kernels, shards(): pl.pallas_call(store, out_shape=results, in_specs=[vmem, vmem], out_specs...  2.06 us
    unnamed x4, local copies, waits for them, and re-layouts  1.52 us

profile of v3, /device:TPU:0, one launch (start us, length us, event | category | flops | bytes accessed | tf_op | source)
XLA Modules:
  0.0 40.2 jit_solution(2266111108366798245)
XLA Ops:
  1.9 34.7 %shard_map.77 = (f32[1,128,1152]{2,1,0:T(8,128)S(1)}, f32[1,64,1152]{2,1,0:T(8,128)S(1)}) custom-call(f32[1]{0:T(128)} %bitcast.2.scale_ref, f32[1]{0:T(128)} %bitcast.3.shift_ref, s32[1,128]{1,0:T(1,128)} %label_ref.1, bf16[1,128,1152]{2,1,0:T(8,128)(2,1)} %image_ref.1, bf16[1,128,1152]{2,1,0:T(8,128)(2,1)} %feat_ref.1, bf16[1152,1152]{1,0:T(8,128)(2,1)} %head_ref.1), custom_call_target="tpu_custom_call" | custom-call | tf_op jit(solution)/shard_map/pallas_call | solution.py:448
  36.6 0.0 copy-start
  36.6 0.8 %copy-done = f32[1,128,1152]{2,1,0:T(8,128)} copy-done((f32[1,128,1152]{2,1,0:T(8,128)}, f32[1,128,1152]{2,1,0:T(8,128)S(1)}, u32[]{:S(2)}) %copy-start) | copy-done | bytes 589848
  37.4 0.0 copy-start.1
  37.4 0.7 %copy-done.1 = f32[1,64,1152]{2,1,0:T(8,128)} copy-done((f32[1,64,1152]{2,1,0:T(8,128)}, f32[1,64,1152]{2,1,0:T(8,128)S(1)}, u32[]{:S(2)}) %copy-start.1) | copy-done | bytes 294936
  38.1 2.1 %shard_map.78 = (f32[1,128,1152]{2,1,0:T(8,128)}, f32[1,64,1152]{2,1,0:T(8,128)}) custom-call(f32[1,128,1152]{2,1,0:T(8,128)} %copy-done, f32[1,64,1152]{2,1,0:T(8,128)} %copy-done.1), custom_call_target="tpu_custom_call" | custom-call | tf_op jit(solution)/shard_map/pallas_call | solution.py:493
Async XLA Ops:
  36.6 0.8 %copy-start = (f32[1,128,1152]{2,1,0:T(8,128)}, f32[1,128,1152]{2,1,0:T(8,128)S(1)}, u32[]{:S(2)}) copy-start(f32[1,128,1152]{2,1,0:T(8,128)S(1)} %get-tuple-element.4.feat_v) | copy-start | bytes 1769476
  37.4 0.7 %copy-start.1 = (f32[1,64,1152]{2,1,0:T(8,128)}, f32[1,64,1152]{2,1,0:T(8,128)S(1)}, u32[]{:S(2)}) copy-start(f32[1,64,1152]{2,1,0:T(8,128)S(1)} %get-tuple-element.5.image_v) | copy-start | bytes 884740

commit v4 on v3

--- a/solution.py
+++ b/solution.py
@@ -51,11 +51,12 @@
 
 STEPS = 4
 COPIES = 1 + 2 * STEPS
+LAG = 3
 
 
 class Line:
     def __init__(self, refs, owner, label_row, pieces):
-        self.label_out, self.label_in, self.pair_in, self.table_out, self.table_in, self.send, self.recv = refs
+        self.label_out, self.label_in, self.pair_in, self.table_out, self.table_in, self.hot, self.send, self.recv = refs
         self.label_row = label_row
         self.images = self.table_out.shape[1]
         self.pieces = pieces
@@ -88,12 +89,28 @@
         at = 1 + (1 + slot) * self.count + k
         return self.copy(at, self.table_out.at[part], self.table_in.at[part], device)
 
-    def tables(self, label_row, devices, values):
-        rows = label_row.shape[1]
-        ids = lax.broadcasted_iota(jnp.int32, (self.images, rows), 0).astype(jnp.float32)
-        firsts = [(d * self.images).astype(jnp.float32) for d in devices]
-        hot = jnp.concatenate([jnp.where(ids + f == label_row, 1.0, 0.0) for f in firsts], axis=0)
-        return jnp.dot(hot.astype(jnp.bfloat16), values, preferred_element_type=jnp.float32)
+    def mark(self, at, label_row, devices):
+        images, rows = self.images, label_row.shape[1]
+        ids = lax.broadcasted_iota(jnp.int32, (images, rows), 0).astype(jnp.float32)
+        for i, device in enumerate(devices):
+            hot = jnp.where(ids + (device * images).astype(jnp.float32) == label_row, 1.0, 0.0)
+            self.hot[pl.ds((at + i) * images, images)] = hot.astype(jnp.bfloat16)
+
+    def tables(self, at, count, values):
+        hot = self.hot[pl.ds(at * self.images, count * self.images)]
+        return jnp.dot(hot, values, preferred_element_type=jnp.float32)
+
+    def prepare(self):
+        @pl.when(self.is_end)
+        def _():
+            self.mark(0, self.label_row, [self.owner])
+
+        @pl.when(self.is_inner)
+        def _():
+            devices = [self.far_inner, self.far_end, self.owner]
+            self.mark(0, self.label_row, [self.end] + devices)
+            self.labels.wait_recv()
+            self.mark(4, self.label_in[pl.ds(0, 1)], devices)
 
     def send_labels(self):
         @pl.when(self.is_end)
@@ -106,14 +123,12 @@
         @pl.when(self.is_end)
         def _():
             self.rows_copy(pair_v, k).start()
-            d_image_ref[0, :, part] = self.tables(self.label_row, [self.owner], pair_v[:, part])
+            d_image_ref[0, :, part] = self.tables(0, 1, pair_v[:, part])
 
         @pl.when(self.is_inner)
         def _():
-            self.table_out[0, :, part] = self.tables(self.label_row, [self.end], pair_v[:, part]).astype(jnp.bfloat16)
+            self.table_out[0, :, part] = self.tables(0, 1, pair_v[:, part]).astype(jnp.bfloat16)
             self.table_copy(0, k).start()
-            if k == 0:
-                self.labels.wait_recv()
 
     def step(self, pair_v, k, d_image_ref):
         images = self.images
@@ -121,10 +136,9 @@
 
         @pl.when(self.is_inner)
         def _():
-            devices = [self.far_inner, self.far_end, self.owner]
-            sums = self.tables(self.label_row, devices, pair_v[:, part])
+            sums = self.tables(1, 3, pair_v[:, part])
             self.rows_copy(pair_v, k).wait_recv()
-            sums = sums + self.tables(self.label_in[pl.ds(0, 1)], devices, self.pair_in[:, part])
+            sums = sums + self.tables(4, 3, self.pair_in[:, part])
             for slot in (1, 2):
                 self.table_out[slot, :, part] = sums[(slot - 1) * images : slot * images].astype(jnp.bfloat16)
                 self.table_copy(slot, k).start()
@@ -180,6 +194,9 @@
     def send_labels(self):
         pass
 
+    def prepare(self):
+        pass
+
     def ready(self, pair_v, k, d_image_ref):
         if k + 1 < len(pieces_of(pair_v.shape[1])):
             return
@@ -200,11 +217,7 @@
 
 
 def pieces_of(width):
-    lanes = width // 128
-    small = max(lanes // 4, 1)
-    sizes = [lanes - 3 * small] + [small] * 3 if lanes > 3 * small else [lanes]
-    starts = [sum(sizes[:i]) for i in range(len(sizes))]
-    return [(128 * a, 128 * b) for a, b in zip(starts, sizes)]
+    return [(first, 128) for first in range(0, width, 128)]
 
 
 def kernel(
@@ -249,15 +262,6 @@
     me = lax.axis_index("loop")
     owner = lax.axis_index("dp")
 
-    load_image = pltpu.make_async_copy(image_ref.at[0], image_v, load_sem.at[0])
-    load_feat = pltpu.make_async_copy(feat_ref.at[0], feat_v, load_sem.at[1])
-    load_head = pltpu.make_async_copy(head_ref, head_v, load_sem.at[2])
-    load_label = pltpu.make_async_copy(label_ref, label_v, load_sem.at[3])
-    load_label.start()
-    load_image.start()
-    load_feat.start()
-    load_head.start()
-
     barrier = pltpu.get_barrier_semaphore()
     for mask in (CORE, NEAR, FAR):
         pl.semaphore_signal(
@@ -271,6 +275,15 @@
             device_id_type=pl.DeviceIdType.MESH,
         )
 
+    load_image = pltpu.make_async_copy(image_ref.at[0], image_v, load_sem.at[0])
+    load_feat = pltpu.make_async_copy(feat_ref.at[0], feat_v, load_sem.at[1])
+    load_head = pltpu.make_async_copy(head_ref, head_v, load_sem.at[2])
+    load_label = pltpu.make_async_copy(label_ref, label_v, load_sem.at[3])
+    load_label.start()
+    load_image.start()
+    load_feat.start()
+    load_head.start()
+
     scale = scale_ref[0]
     shift = shift_ref[0]
     load_label.wait()
@@ -306,17 +319,16 @@
     inv_x = lax.rsqrt(jnp.sum(image * image, axis=-1, keepdims=True) + EPS)
     xbuf[pl.ds(0, rows)] = (image * inv_x).astype(jnp.bfloat16)
 
-    pl.semaphore_wait(barrier, 3 + owners - 1)
-    xs.start()
-    sums.send_labels()
-
     load_feat.wait()
     load_head.wait()
     text_pre = jnp.dot(feat_v[...], head_v[...], preferred_element_type=jnp.float32)
     inv_y = lax.rsqrt(jnp.sum(text_pre * text_pre, axis=-1, keepdims=True) + EPS)
     unit_y = text_pre * inv_y
     ybuf[pl.ds(0, rows)] = unit_y.astype(jnp.bfloat16)
+    pl.semaphore_wait(barrier, 3 + owners - 1)
     ys.start()
+    xs.start()
+    sums.send_labels()
     unit_y_v[...] = unit_y
 
     def weights(mine, first, count, other, block, blocks, weight):
@@ -376,6 +388,7 @@
     weights(ybuf, 0, 1, xbuf, 3, 1, y_weight)
     for c in columns:
         text_v[c] = product(y_weight, 0, xbuf, c)
+    sums.prepare()
     dots_copy.wait_recv()
     there = jnp.broadcast_to(dots_in[pl.ds(0, 1)], (rows, rows)).T[:, :1]
     along = scale * (own_dots + there)
@@ -386,9 +399,11 @@
         grad = scale * (grad + x_in[c].astype(jnp.float32))
         d_pair_v[c] = ((grad - unit_x * along) * inv_x).astype(jnp.bfloat16)
         sums.ready(d_pair_v, k, d_image_ref)
-        if k > 0:
-            sums.step(d_pair_v, k - 1, d_image_ref)
-
+        if k >= LAG:
+            sums.step(d_pair_v, k - LAG, d_image_ref)
+
+    for k in range(len(pieces) - LAG, len(pieces) - 1):
+        sums.step(d_pair_v, k, d_image_ref)
     for c in y_parts:
         c.wait_recv()
     grad = scale * (text_v[...] + y_in[...].astype(jnp.float32))
@@ -431,6 +446,7 @@
             pltpu.VMEM((rows, width), jnp.bfloat16),
             pltpu.VMEM((3, images, width), jnp.bfloat16),
             pltpu.VMEM((3, images, width), jnp.bfloat16),
+            pltpu.VMEM((7 * images, rows), jnp.bfloat16),
             dma((1 + 4 * count,)),
             dma((1 + 4 * count,)),
         ]
@@ -496,6 +512,7 @@
         in_specs=[vmem, vmem],
         out_specs=(hbm, hbm),
         scratch_shapes=[dma((2,))],
+        compiler_params=pltpu.CompilerParams(vmem_limit_bytes=4 * 1024 * 1024),
     )(*gradients)
 
 

time: 40.4 us -> 37.5 us (0.928)
  local copies, waits for them, and re-layouts: 1.52 us -> 0 us
  Pallas kernels: 36.7 us -> 35.3 us
    unnamed x4 -> x0, local copies, waits for them, and re-layouts: 1.52 us -> none
    pallas_call x1, Pallas kernels: 2.06 us -> 0.93 us  [shards(): pl.pallas_call(store, out_shape=results, in_specs=[vmem, vmem], out_specs...]
where the time goes in v4:
time: 37.5 us; the launch traced here: 37.3 us
  Pallas kernels  35.3 us (94%)
  between operations  1.93 us (5%)
    pallas_call x1, Pallas kernels, shards(): pl.pallas_call(functools.partial(kernel, owners), out_shape=results, in_s...  34.4 us
    pallas_call x1, Pallas kernels, shards(): pl.pallas_call(store, out_shape=results, in_specs=[vmem, vmem], out_specs...  0.93 us

profile of v4, /device:TPU:0, one launch (start us, length us, event | category | flops | bytes accessed | tf_op | source)
XLA Modules:
  0.0 37.3 jit_solution(7734102660920643371)
XLA Ops:
  1.9 34.4 %shard_map.77 = (f32[1,128,1152]{2,1,0:T(8,128)S(1)}, f32[1,64,1152]{2,1,0:T(8,128)S(1)}) custom-call(f32[1]{0:T(128)} %bitcast.2.scale_ref, f32[1]{0:T(128)} %bitcast.3.shift_ref, s32[1,128]{1,0:T(1,128)} %label_ref.1, bf16[1,128,1152]{2,1,0:T(8,128)(2,1)} %image_ref.1, bf16[1,128,1152]{2,1,0:T(8,128)(2,1)} %feat_ref.1, bf16[1152,1152]{1,0:T(8,128)(2,1)} %head_ref.1), custom_call_target="tpu_custom_call" | custom-call | tf_op jit(solution)/shard_map/pallas_call | solution.py:464
  36.4 0.9 %shard_map.78 = (f32[1,128,1152]{2,1,0:T(8,128)}, f32[1,64,1152]{2,1,0:T(8,128)}) custom-call(f32[1,128,1152]{2,1,0:T(8,128)S(1)} %get-tuple-element.4.feat_v, f32[1,64,1152]{2,1,0:T(8,128)S(1)} %get-tuple-element.5.image_v), custom_call_target="tpu_custom_call" | custom-call | tf_op jit(solution)/shard_map/pallas_call | solution.py:509

commit v5 on v4

--- a/solution.py
+++ b/solution.py
@@ -31,9 +31,9 @@
 
         core, side = partner(me, CORE), partner(me, mask)
         piece = rows // STEPS
-        self.own_core = copy(0, 0, 2, core, 0, rows)
-        self.direct = [copy(1 + i, 0, 1, side, i * piece, piece) for i in range(STEPS)]
-        self.relay = [copy(1 + STEPS + i, 1, 3, core, i * piece, piece) for i in range(STEPS)]
+        self.own_core = copy(0, 0, 1, core, 0, rows)
+        self.direct = [copy(1 + i, 0, 2, side, i * piece, piece) for i in range(STEPS)]
+        self.relay = [copy(1 + STEPS + i, 2, 3, core, i * piece, piece) for i in range(STEPS)]
 
     def start(self):
         for c in self.direct:
@@ -51,7 +51,7 @@
 
 STEPS = 4
 COPIES = 1 + 2 * STEPS
-LAG = 3
+LAG = 2
 
 
 class Line:
@@ -217,7 +217,9 @@
 
 
 def pieces_of(width):
-    return [(first, 128) for first in range(0, width, 128)]
+    lanes = width // 128
+    sizes = [1] + [2] * ((lanes - 3) // 2) + [1] * (2 - lanes % 2 + 1) if lanes > 3 else [1] * lanes
+    return [(128 * sum(sizes[:i]), 128 * size) for i, size in enumerate(sizes)]
 
 
 def kernel(
@@ -240,6 +242,7 @@
     y_weight,
     unit_y_v,
     text_v,
+    image_grad_v,
     d_pair_v,
     x_out,
     x_in,
@@ -331,85 +334,90 @@
     sums.send_labels()
     unit_y_v[...] = unit_y
 
-    def weights(mine, first, count, other, block, blocks, weight):
+    def weights(mine, row, other, block, blocks, weight):
         dots = lax.dot_general(
-            mine[pl.ds(first * rows, count * rows)],
+            mine[pl.ds(row * 2 * rows, rows)],
             other[pl.ds(block * rows, blocks * rows)],
             NT,
             preferred_element_type=jnp.float32,
         )
         logits = scale * dots + shift
-        if first == 0 and block == 0:
-            value = jax.nn.sigmoid(jnp.where(same, -logits, logits))
-            value = jnp.where(same, -value, value)
+        if row == 0 and block == 0:
+            flip = jnp.concatenate([same, jnp.zeros_like(same)], axis=1)
+            value = jax.nn.sigmoid(jnp.where(flip, -logits, logits))
+            value = jnp.where(flip, -value, value)
         else:
             value = jax.nn.sigmoid(logits)
         value = value.astype(jnp.bfloat16)
-        weight[pl.ds(first * rows, count * rows), pl.ds(block * rows, blocks * rows)] = value
-        return jnp.sum(value.astype(jnp.float32) * dots, axis=-1, keepdims=True)
-
-    def product(weight, first, buf, column):
-        return jnp.dot(weight[pl.ds(first * rows, rows)], buf[column], preferred_element_type=jnp.float32)
-
-    xs.hand_on(0)
+        weight[pl.ds(row * rows, rows), pl.ds(block * rows, blocks * rows)] = value
+        return value.astype(jnp.float32) * dots
+
+    def product(weight, row, buf, column):
+        return jnp.dot(weight[pl.ds(row * rows, rows)], buf[column], preferred_element_type=jnp.float32)
+
+    everything = (slice(None), slice(None))
+
     ys.own_core.wait_recv()
     xs.own_core.wait_recv()
-    own_dots = weights(xbuf, 0, 1, ybuf, 0, 1, x_weight) + weights(xbuf, 0, 1, ybuf, 2, 1, x_weight)
-    weights(ybuf, 0, 1, xbuf, 0, 1, y_weight)
-    weights(ybuf, 0, 1, xbuf, 2, 1, y_weight)
-    xs.hand_on(1)
+    own_dots = weights(xbuf, 0, ybuf, 0, 2, x_weight)
     ys.hand_on(0)
-    xs.hand_on(2)
-    ys.hand_on(1)
-    xs.hand_on(3)
-    ys.hand_on(2)
-    near_dots = weights(xbuf, 1, 1, ybuf, 0, 1, x_weight) + weights(xbuf, 1, 1, ybuf, 2, 1, x_weight)
-    ys.hand_on(3)
-
-    near_dots = near_dots + weights(xbuf, 1, 1, ybuf, 1, 1, x_weight)
+    xs.hand_on(0)
+    weights(ybuf, 0, xbuf, 0, 2, y_weight)
+    for i in range(1, STEPS):
+        ys.hand_on(i)
+        xs.hand_on(i)
+    near_dots = weights(xbuf, 1, ybuf, 0, 2, x_weight)
+
     for c in ys.relay:
         c.wait_recv()
-    near_dots = near_dots + weights(xbuf, 1, 1, ybuf, 3, 1, x_weight)
+    near_dots = jnp.sum(near_dots + weights(xbuf, 1, ybuf, 2, 2, x_weight), axis=-1, keepdims=True)
     dots_out[...] = jnp.broadcast_to(near_dots, (rows, rows)).T[:8]
     dots_copy.start()
-    for k, c in enumerate(columns):
-        x_out[c] = product(x_weight, 1, ybuf, c).astype(jnp.bfloat16)
-        x_parts[k].start()
-
-    for c in xs.relay:
-        c.wait_recv()
-    weights(ybuf, 1, 1, xbuf, 0, 4, y_weight)
-    for k, c in enumerate(columns):
-        y_out[c] = product(y_weight, 1, xbuf, c).astype(jnp.bfloat16)
-        y_parts[k].start()
-
-    own_dots = own_dots + weights(xbuf, 0, 1, ybuf, 1, 1, x_weight) + weights(xbuf, 0, 1, ybuf, 3, 1, x_weight)
-    weights(ybuf, 0, 1, xbuf, 1, 1, y_weight)
-    weights(ybuf, 0, 1, xbuf, 3, 1, y_weight)
-    for c in columns:
-        text_v[c] = product(y_weight, 0, xbuf, c)
+    for first in range(0, len(pieces), 2):
+        pair = pieces[first : first + 2]
+        part = (slice(None), pl.ds(pair[0][0], sum(size for _, size in pair)))
+        x_out[part] = product(x_weight, 1, ybuf, part).astype(jnp.bfloat16)
+        for c in x_parts[first : first + 2]:
+            c.start()
+
+    own_dots = jnp.sum(own_dots + weights(xbuf, 0, ybuf, 2, 2, x_weight), axis=-1, keepdims=True)
+    image_grad_v[...] = product(x_weight, 0, ybuf, everything)
     sums.prepare()
     dots_copy.wait_recv()
     there = jnp.broadcast_to(dots_in[pl.ds(0, 1)], (rows, rows)).T[:, :1]
     along = scale * (own_dots + there)
+
+    def far_texts():
+        for c in xs.relay:
+            c.wait_recv()
+        weights(ybuf, 1, xbuf, 0, 4, y_weight)
+        y_out[...] = product(y_weight, 1, xbuf, everything).astype(jnp.bfloat16)
+        for c in y_parts:
+            c.start()
+
+    def own_texts():
+        weights(ybuf, 0, xbuf, 2, 2, y_weight)
+        text_v[...] = product(y_weight, 0, xbuf, everything)
+
+    fill = {1: far_texts, len(pieces) - 3: own_texts}
     for k, c in enumerate(columns):
-        grad = product(x_weight, 0, ybuf, c)
         unit_x = image_v[c].astype(jnp.float32) * inv_x
         x_parts[k].wait_recv()
-        grad = scale * (grad + x_in[c].astype(jnp.float32))
+        grad = scale * (image_grad_v[c] + x_in[c].astype(jnp.float32))
         d_pair_v[c] = ((grad - unit_x * along) * inv_x).astype(jnp.bfloat16)
         sums.ready(d_pair_v, k, d_image_ref)
+        if k in fill:
+            fill[k]()
         if k >= LAG:
             sums.step(d_pair_v, k - LAG, d_image_ref)
 
-    for k in range(len(pieces) - LAG, len(pieces) - 1):
+    for k in range(len(pieces) - LAG, len(pieces)):
         sums.step(d_pair_v, k, d_image_ref)
     for c in y_parts:
         c.wait_recv()
     grad = scale * (text_v[...] + y_in[...].astype(jnp.float32))
     unit_y = unit_y_v[...]
     d_text = (grad - unit_y * jnp.sum(unit_y * grad, axis=-1, keepdims=True)) * inv_y
-    sums.step(d_pair_v, len(pieces) - 1, d_image_ref)
     d_feat_ref[0] = lax.dot_general(
         d_text.astype(jnp.bfloat16), head_v[...], NT, preferred_element_type=jnp.float32
     )
@@ -475,6 +483,7 @@
             pltpu.VMEM((4 * rows, width), jnp.bfloat16),
             pltpu.VMEM((2 * rows, 4 * rows), jnp.bfloat16),
             pltpu.VMEM((2 * rows, 4 * rows), jnp.bfloat16),
+            pltpu.VMEM((rows, width), jnp.float32),
             pltpu.VMEM((rows, width), jnp.float32),
             pltpu.VMEM((rows, width), jnp.float32),
             pltpu.VMEM((rows, width), jnp.bfloat16),

time: 37.5 us -> 36.6 us (0.976)
  Pallas kernels: 35.3 us -> 34.5 us
    pallas_call x1, Pallas kernels: 34.4 us -> 33.6 us  [shards(): pl.pallas_call(functools.partial(kernel, owners), out_shape=results, in_s...]
where the time goes in v5:
time: 36.6 us; the launch traced here: 36.4 us
  Pallas kernels  34.5 us (94%)
  between operations  1.93 us (5%)
    pallas_call x1, Pallas kernels, shards(): pl.pallas_call(functools.partial(kernel, owners), out_shape=results, in_s...  33.6 us
    pallas_call x1, Pallas kernels, shards(): pl.pallas_call(store, out_shape=results, in_specs=[vmem, vmem], out_specs...  0.93 us

profile of v5, /device:TPU:0, one launch (start us, length us, event | category | flops | bytes accessed | tf_op | source)
XLA Modules:
  0.0 36.4 jit_solution(14782708761253518073)
XLA Ops:
  1.9 33.6 %shard_map.77 = (f32[1,128,1152]{2,1,0:T(8,128)S(1)}, f32[1,64,1152]{2,1,0:T(8,128)S(1)}) custom-call(f32[1]{0:T(128)} %bitcast.2.scale_ref, f32[1]{0:T(128)} %bitcast.3.shift_ref, s32[1,128]{1,0:T(1,128)} %label_ref.1, bf16[1,128,1152]{2,1,0:T(8,128)(2,1)} %image_ref.1, bf16[1,128,1152]{2,1,0:T(8,128)(2,1)} %feat_ref.1, bf16[1152,1152]{1,0:T(8,128)(2,1)} %head_ref.1), custom_call_target="tpu_custom_call" | custom-call | tf_op jit(solution)/shard_map/pallas_call | solution.py:472
  35.5 0.9 %shard_map.78 = (f32[1,128,1152]{2,1,0:T(8,128)}, f32[1,64,1152]{2,1,0:T(8,128)}) custom-call(f32[1,128,1152]{2,1,0:T(8,128)S(1)} %get-tuple-element.4.feat_v, f32[1,64,1152]{2,1,0:T(8,128)S(1)} %get-tuple-element.5.image_v), custom_call_target="tpu_custom_call" | custom-call | tf_op jit(solution)/shard_map/pallas_call | solution.py:518

commit v6 on v5

--- a/solution.py
+++ b/solution.py
@@ -250,6 +250,8 @@
     y_in,
     dots_out,
     dots_in,
+    text_dots_out,
+    text_dots_in,
     load_sem,
     x_send,
     x_recv,
@@ -316,6 +318,7 @@
     x_parts = [side_copy(x_out.at[c], x_in.at[c], px_send, px_recv, k, NEAR) for k, c in enumerate(columns)]
     y_parts = [side_copy(y_out.at[c], y_in.at[c], py_send, py_recv, k, FAR) for k, c in enumerate(columns)]
     dots_copy = side_copy(dots_out, dots_in, px_send, px_recv, len(pieces), NEAR)
+    text_dots_copy = side_copy(text_dots_out, text_dots_in, py_send, py_recv, len(pieces), FAR)
 
     load_image.wait()
     image = image_v[...].astype(jnp.float32)
@@ -362,11 +365,12 @@
     own_dots = weights(xbuf, 0, ybuf, 0, 2, x_weight)
     ys.hand_on(0)
     xs.hand_on(0)
-    weights(ybuf, 0, xbuf, 0, 2, y_weight)
+    own_text_dots = [weights(ybuf, 0, xbuf, 0, 2, y_weight)]
     for i in range(1, STEPS):
         ys.hand_on(i)
         xs.hand_on(i)
     near_dots = weights(xbuf, 1, ybuf, 0, 2, x_weight)
+    far_dots = weights(ybuf, 1, xbuf, 0, 2, y_weight)
 
     for c in ys.relay:
         c.wait_recv()
@@ -390,13 +394,18 @@
     def far_texts():
         for c in xs.relay:
             c.wait_recv()
-        weights(ybuf, 1, xbuf, 0, 4, y_weight)
-        y_out[...] = product(y_weight, 1, xbuf, everything).astype(jnp.bfloat16)
-        for c in y_parts:
-            c.start()
+        dots = jnp.sum(far_dots + weights(ybuf, 1, xbuf, 2, 2, y_weight), axis=-1, keepdims=True)
+        text_dots_out[...] = jnp.broadcast_to(dots, (rows, rows)).T[:8]
+        text_dots_copy.start()
+        for first in range(0, len(pieces), 2):
+            pair = pieces[first : first + 2]
+            part = (slice(None), pl.ds(pair[0][0], sum(size for _, size in pair)))
+            y_out[part] = product(y_weight, 1, xbuf, part).astype(jnp.bfloat16)
+            for c in y_parts[first : first + 2]:
+                c.start()
 
     def own_texts():
-        weights(ybuf, 0, xbuf, 2, 2, y_weight)
+        own_text_dots.append(weights(ybuf, 0, xbuf, 2, 2, y_weight))
         text_v[...] = product(y_weight, 0, xbuf, everything)
 
     fill = {1: far_texts, len(pieces) - 3: own_texts}
@@ -411,21 +420,26 @@
         if k >= LAG:
             sums.step(d_pair_v, k - LAG, d_image_ref)
 
-    for k in range(len(pieces) - LAG, len(pieces)):
-        sums.step(d_pair_v, k, d_image_ref)
-    for c in y_parts:
-        c.wait_recv()
-    grad = scale * (text_v[...] + y_in[...].astype(jnp.float32))
-    unit_y = unit_y_v[...]
-    d_text = (grad - unit_y * jnp.sum(unit_y * grad, axis=-1, keepdims=True)) * inv_y
-    d_feat_ref[0] = lax.dot_general(
-        d_text.astype(jnp.bfloat16), head_v[...], NT, preferred_element_type=jnp.float32
-    )
+    text_dots_copy.wait_recv()
+    there = jnp.broadcast_to(text_dots_in[pl.ds(0, 1)], (rows, rows)).T[:, :1]
+    along = scale * (jnp.sum(own_text_dots[0] + own_text_dots[1], axis=-1, keepdims=True) + there)
+    steps = {2 * i: len(pieces) - LAG + i for i in range(LAG)}
+    for k, c in enumerate(columns):
+        y_parts[k].wait_recv()
+        grad = scale * (text_v[c] + y_in[c].astype(jnp.float32))
+        d_text = ((grad - unit_y_v[c] * along) * inv_y).astype(jnp.bfloat16)
+        term = lax.dot_general(d_text, head_v[c], NT, preferred_element_type=jnp.float32)
+        if k == 0:
+            d_feat_ref[0] = term
+        else:
+            d_feat_ref[0] += term
+        if k in steps:
+            sums.step(d_pair_v, steps[k], d_image_ref)
 
     sums.last(d_pair_v, d_image_ref)
     xs.drain()
     ys.drain()
-    for c in x_parts + y_parts + [dots_copy]:
+    for c in x_parts + y_parts + [dots_copy, text_dots_copy]:
         c.wait_send()
 
 
@@ -493,6 +507,8 @@
             pltpu.VMEM((rows, width), jnp.bfloat16),
             pltpu.VMEM((8, rows), jnp.float32),
             pltpu.VMEM((8, rows), jnp.float32),
+            pltpu.VMEM((8, rows), jnp.float32),
+            pltpu.VMEM((8, rows), jnp.float32),
             dma((4,)),
             dma((COPIES,)),
             dma((COPIES,)),
@@ -500,8 +516,8 @@
             dma((COPIES,)),
             dma((count + 1,)),
             dma((count + 1,)),
-            dma((count,)),
-            dma((count,)),
+            dma((count + 1,)),
+            dma((count + 1,)),
             *dp_scratch,
         ],
         compiler_params=pltpu.CompilerParams(

time: 36.6 us -> 37 us (1.011)
  Pallas kernels: 34.5 us -> 34.9 us
    pallas_call x1, Pallas kernels: 33.6 us -> 34 us  [shards(): pl.pallas_call(functools.partial(kernel, owners), out_shape=results, in_s...]
where the time goes in v6:
time: 37 us; the launch traced here: 36.8 us
  Pallas kernels  34.9 us (94%)
  between operations  1.93 us (5%)
    pallas_call x1, Pallas kernels, shards(): pl.pallas_call(functools.partial(kernel, owners), out_shape=results, in_s...  34 us
    pallas_call x1, Pallas kernels, shards(): pl.pallas_call(store, out_shape=results, in_specs=[vmem, vmem], out_specs...  0.93 us

profile of v6, /device:TPU:0, one launch (start us, length us, event | category | flops | bytes accessed | tf_op | source)
XLA Modules:
  0.0 36.8 jit_solution(9100705470539951882)
XLA Ops:
  1.9 34.0 %shard_map.77 = (f32[1,128,1152]{2,1,0:T(8,128)S(1)}, f32[1,64,1152]{2,1,0:T(8,128)S(1)}) custom-call(f32[1]{0:T(128)} %bitcast.2.scale_ref, f32[1]{0:T(128)} %bitcast.3.shift_ref, s32[1,128]{1,0:T(1,128)} %label_ref.1, bf16[1,128,1152]{2,1,0:T(8,128)(2,1)} %image_ref.1, bf16[1,128,1152]{2,1,0:T(8,128)(2,1)} %feat_ref.1, bf16[1152,1152]{1,0:T(8,128)(2,1)} %head_ref.1), custom_call_target="tpu_custom_call" | custom-call | tf_op jit(solution)/shard_map/pallas_call | solution.py:486
  35.9 0.9 %shard_map.78 = (f32[1,128,1152]{2,1,0:T(8,128)}, f32[1,64,1152]{2,1,0:T(8,128)}) custom-call(f32[1,128,1152]{2,1,0:T(8,128)S(1)} %get-tuple-element.4.feat_v, f32[1,64,1152]{2,1,0:T(8,128)S(1)} %get-tuple-element.5.image_v), custom_call_target="tpu_custom_call" | custom-call | tf_op jit(solution)/shard_map/pallas_call | solution.py:534

commit v7 on v5

--- a/solution.py
+++ b/solution.py
@@ -322,16 +322,17 @@
     inv_x = lax.rsqrt(jnp.sum(image * image, axis=-1, keepdims=True) + EPS)
     xbuf[pl.ds(0, rows)] = (image * inv_x).astype(jnp.bfloat16)
 
+    pl.semaphore_wait(barrier, 3 + owners - 1)
+    xs.start()
+    sums.send_labels()
+
     load_feat.wait()
     load_head.wait()
     text_pre = jnp.dot(feat_v[...], head_v[...], preferred_element_type=jnp.float32)
     inv_y = lax.rsqrt(jnp.sum(text_pre * text_pre, axis=-1, keepdims=True) + EPS)
     unit_y = text_pre * inv_y
     ybuf[pl.ds(0, rows)] = unit_y.astype(jnp.bfloat16)
-    pl.semaphore_wait(barrier, 3 + owners - 1)
     ys.start()
-    xs.start()
-    sums.send_labels()
     unit_y_v[...] = unit_y
 
     def weights(mine, row, other, block, blocks, weight):
@@ -364,8 +365,8 @@
     xs.hand_on(0)
     weights(ybuf, 0, xbuf, 0, 2, y_weight)
     for i in range(1, STEPS):
+        xs.hand_on(i)
         ys.hand_on(i)
-        xs.hand_on(i)
     near_dots = weights(xbuf, 1, ybuf, 0, 2, x_weight)
 
     for c in ys.relay:

time: 36.6 us -> 36.6 us (level)
  no operation moved by 1% of the time
where the time goes in v7:
time: 36.6 us; the launch traced here: 36.4 us
  Pallas kernels  34.5 us (94%)
  between operations  1.93 us (5%)
    pallas_call x1, Pallas kernels, shards(): pl.pallas_call(functools.partial(kernel, owners), out_shape=results, in_s...  33.6 us
    pallas_call x1, Pallas kernels, shards(): pl.pallas_call(store, out_shape=results, in_specs=[vmem, vmem], out_specs...  0.93 us

profile of v7, /device:TPU:0, one launch (start us, length us, event | category | flops | bytes accessed | tf_op | source)
XLA Modules:
  0.0 36.4 jit_solution(10277956856581275172)
XLA Ops:
  1.9 33.6 %shard_map.77 = (f32[1,128,1152]{2,1,0:T(8,128)S(1)}, f32[1,64,1152]{2,1,0:T(8,128)S(1)}) custom-call(f32[1]{0:T(128)} %bitcast.2.scale_ref, f32[1]{0:T(128)} %bitcast.3.shift_ref, s32[1,128]{1,0:T(1,128)} %label_ref.1, bf16[1,128,1152]{2,1,0:T(8,128)(2,1)} %image_ref.1, bf16[1,128,1152]{2,1,0:T(8,128)(2,1)} %feat_ref.1, bf16[1152,1152]{1,0:T(8,128)(2,1)} %head_ref.1), custom_call_target="tpu_custom_call" | custom-call | tf_op jit(solution)/shard_map/pallas_call | solution.py:473
  35.5 0.9 %shard_map.78 = (f32[1,128,1152]{2,1,0:T(8,128)}, f32[1,64,1152]{2,1,0:T(8,128)}) custom-call(f32[1,128,1152]{2,1,0:T(8,128)S(1)} %get-tuple-element.4.feat_v, f32[1,64,1152]{2,1,0:T(8,128)S(1)} %get-tuple-element.5.image_v), custom_call_target="tpu_custom_call" | custom-call | tf_op jit(solution)/shard_map/pallas_call | solution.py:519
